TPU v7x, 128 devices: a whole 4x4x4 slice. The times are simulated.
128 devices in a mesh: dp: 32 (over x, y, core), tensor: 4 (over z).
Axes of the slice: x: 4, y: 4, z: 4, core: 2. Of those that a mesh axis runs over, the one named last changes fastest.
Arguments:
- grads_local: bfloat16 [32, 2, 8192, 1024], P('dp', None, None, 'tensor'), may hold values from -6 to 6
- params: float32 [2, 8192, 1024], P(None, 'dp', 'tensor'), may hold values from -6 to 6
- moments: float32 [3, 2, 8192, 1024], P(None, None, 'dp', 'tensor'), may hold values from -6 to 6
- row_stat: float32 [2, 8192], P(None, 'dp'), may hold values from 0.1 to 10
- col_stat: float32 [2, 1024], P(None, 'tensor'), may hold values from 0.1 to 10
- lstm_hidden: float32 [2, 512], replicated, may hold values from -0.9 to 0.9
- lstm_cell: float32 [2, 512], replicated, may hold values from -4 to 4
- lstm_input_w: float32 [5, 2048], replicated, may hold values from -2.5 to 2.5
- lstm_recur_w: float32 [512, 2048], replicated, may hold values from -0.25 to 0.25
- lstm_bias: float32 [2048], replicated, may hold values from -3 to 3
- head_w: float32 [512, 34], replicated, may hold values from -0.25 to 0.25
- head_bias: float32 [34], replicated, may hold values from -2.5 to 2.5
- mlp_first: float32 [6, 32], replicated, may hold values from -2.5 to 2.5
- mlp_second: float32 [32, 2], replicated, may hold values from -1 to 1
Outputs:
- new_params: float32 [2, 8192, 1024], P(None, 'dp', 'tensor')
- new_moments: float32 [3, 2, 8192, 1024], P(None, None, 'dp', 'tensor')
- new_rows: float32 [2, 8192], P(None, 'dp')
- new_cols: float32 [2, 1024], P(None, 'tensor')
- new_hidden: float32 [2, 512], replicated
- new_cell: float32 [2, 512], replicated
All inputs are finite; a program needn't handle non-finite values.
Results may differ from a plain program's by a relative error of at most 0.0003.
Values sent between devices are 32-bit elements; how exact they have to be, the bound alone decides.
A program may use at most 128 MiB of HBM per device.

v0:
```python
import jax
import jax.numpy as jnp
from jax import lax
from jax.sharding import PartitionSpec as P

D = 8192
KV = 1024
HID = 32


HIGH = lax.Precision.HIGHEST


def lstm_step(features, hidden, cell, input_w, recur_w, bias):
    gates = (
        jnp.dot(features, input_w, precision=HIGH) + jnp.dot(hidden, recur_w, precision=HIGH) + bias
    )
    width = hidden.shape[1]
    in_gate = jax.nn.sigmoid(gates[:, :width])
    forget = jax.nn.sigmoid(gates[:, width : 2 * width])
    candidate = jnp.tanh(gates[:, 2 * width : 3 * width])
    out_gate = jax.nn.sigmoid(gates[:, 3 * width :])
    cell_next = forget * cell + in_gate * candidate
    return (out_gate * jnp.tanh(cell_next), cell_next)


def process(contrib, params, moments, rows, cols, hidden, cell, weights):
    input_w, recur_w, gate_bias, head_w, head_bias, mlp_first, mlp_second = weights
    grad = lax.psum_scatter(contrib[0].astype(jnp.float32), "dp", scatter_dimension=1, tiled=True)
    decays = jnp.array([0.5, 0.9, 0.99], jnp.float32)[:, None, None, None]
    moments_new = decays * moments + (1.0 - decays) * grad[None]
    squares = grad * grad
    row_part = jnp.sum(squares, 2)
    col_part = jnp.sum(squares, 1)
    stat_part = jnp.concatenate(
        [
            jnp.sum(row_part, 1)[:, None],
            jnp.sum(moments_new * moments_new, (2, 3)).T,
            jnp.sum(params * params, (1, 2))[:, None],
        ],
        1,
    )
    row_sum = lax.psum(row_part, "tensor")
    col_sum = lax.psum(col_part, "dp")
    stat_sum = lax.psum(stat_part, ("dp", "tensor"))
    rows_new = 0.9 * rows + 0.1 * row_sum / KV
    row_total = lax.psum(jnp.sum(rows_new, 1), "dp")
    cols_new = 0.9 * cols + 0.1 * col_sum / D
    row_mean = row_total / D
    means = stat_sum / (D * KV)
    features = jnp.log(means + 1e-06)
    hidden_new, cell_new = lstm_step(features, hidden, cell, input_w, recur_w, gate_bias)
    modulation = jnp.dot(hidden_new, head_w, precision=HIGH) + head_bias
    net_bias = modulation[:, :HID]
    lr_log = modulation[:, HID]
    mag_scale = modulation[:, HID + 1]
    scale = lax.rsqrt(rows_new[:, :, None] * cols_new[:, None, :] / row_mean[:, None, None] + 1e-08)
    param_norm = lax.rsqrt(means[:, 4] + 1e-06)[:, None, None]
    grad_norm = lax.rsqrt(means[:, 0] + 1e-06)[:, None, None]
    inputs = jnp.stack(
        [
            grad * scale,
            moments_new[0] * scale,
            moments_new[1] * scale,
            moments_new[2] * scale,
            params * param_norm,
            grad * grad_norm,
        ],
        1,
    )
    hidden_units = (
        jnp.einsum("nh,lnrc->lhrc", mlp_first, inputs, precision=HIGH) + net_bias[:, :, None, None]
    )
    hidden_units = jnp.maximum(hidden_units, 0.0)
    outputs = jnp.einsum("ho,lhrc->lorc", mlp_second, hidden_units, precision=HIGH)
    direction = outputs[:, 0]
    magnitude = outputs[:, 1]
    step = (
        jnp.exp(lr_log)[:, None, None]
        * direction
        * jnp.exp(0.5 * mag_scale[:, None, None] * magnitude)
    )
    return (params - step, moments_new, rows_new, cols_new, hidden_new, cell_new)


def body(
    grads_local,
    params,
    moments,
    row_stat,
    col_stat,
    lstm_hidden,
    lstm_cell,
    lstm_input_w,
    lstm_recur_w,
    lstm_bias,
    head_w,
    head_bias,
    mlp_first,
    mlp_second,
):
    weights = (lstm_input_w, lstm_recur_w, lstm_bias, head_w, head_bias, mlp_first, mlp_second)
    return process(
        grads_local, params, moments, row_stat, col_stat, lstm_hidden, lstm_cell, weights
    )


def solution(mesh):
    return jax.shard_map(
        body,
        mesh=mesh,
        in_specs=(
            P("dp", None, None, "tensor"),
            P(None, "dp", "tensor"),
            P(None, None, "dp", "tensor"),
            P(None, "dp"),
            P(None, "tensor"),
            P(),
            P(),
            P(),
            P(),
            P(),
            P(),
            P(),
            P(),
            P(),
        ),
        out_specs=(
            P(None, "dp", "tensor"),
            P(None, None, "dp", "tensor"),
            P(None, "dp"),
            P(None, "tensor"),
            P(),
            P(),
        ),
        check_vma=False,
    )
```

profile of v0, /device:TPU:1, one launch (start us, length us, event | category | flops | bytes accessed | tf_op | source)
XLA Modules:
  0.0 331.8 jit_solution(13046850558787346235)
XLA Ops:
  7.2 0.0 copy-start
  7.2 0.0 reduce-scatter.2.cloned.1.call-start
  7.2 10.4 %bitcast_convert_fusion = f32[2,8192,256]{2,1,0:T(8,128)} fusion(bf16[1,2,8192,256]{3,2,1,0:T(8,128)(2,1)} %param.15), kind=kLoop, calls=%fused_computation.4 | loop fusion | flops 4194304 | bytes 25165824 | tf_op jit(solution)/shard_map/convert_element_type | solution.py:29
  17.7 0.0 copy-start.1
  17.7 0.0 copy-start.13
  17.7 0.0 copy-start.17
  17.7 0.0 reduce-scatter.2.cloned.1.call-update
  17.7 1.0 copy-done.1
  18.7 0.0 copy-start.4
  18.7 0.0 copy-start.9
  18.7 0.2 multiply_reduce_fusion.1
  18.9 0.1 copy.31
  19.0 115.8 %reduce-scatter.2.cloned.1.call-done = f32[2,256,256]{2,1,0:T(8,128)} async-done(((f32[2,8192,256]{2,1,0:T(8,128)}), f32[2,256,256]{2,1,0:T(8,128)}) %reduce-scatter.2.cloned.1.call-update) | async-done | bytes 524304 | tf_op jit(solution)/shard_map/reduce_scatter | solution.py:29
  134.7 1.3 multiply_reduce_fusion.4
  136.0 0.1 copy.30
  136.1 8.9 %psum.29 = f32[2,256]{1,0:T(2,128)S(1)} all-reduce(f32[2,256]{1,0:T(2,128)S(1)} %get-tuple-element.19), channel_id=1, replica_groups=mesh['dp'=32,'tensor'=4] {'tensor'}, use_global_device_ids=true, to_apply=%region_6.0 | all-reduce | flops 512 | bytes 4096 | tf_op jit(solution)/shard_map/psum | solution.py:43
  145.0 0.0 copy-done.13
  145.0 0.1 fusion.36
  145.1 0.0 copy-start.6
  145.1 65.9 %all-reduce = (f32[2]{0:T(128)S(1)}, f32[2,256]{1,0:T(2,128)S(1)}) all-reduce(f32[2]{0:T(128)S(1)} %get-tuple-element.31, f32[2,256]{1,0:T(2,128)S(1)} %get-tuple-element.20), channel_id=1, replica_groups=mesh['dp'=32,'tensor'=4] {'dp'}, use_global_device_ids=true, to_apply=%region_10.0 | all-reduce | flops 514 | bytes 4112 | tf_op jit(solution)/shard_map/psum | solution.py:47
  211.0 0.0 copy-done.16
  211.0 0.0 copy-done.17
  211.0 0.0 copy-start.10
  211.0 0.0 copy-start.15
  211.0 3.0 multiply_reduce_fusion
  214.0 0.0 copy-start.12
  214.0 0.1 pad_maximum_fusion
  214.1 62.0 %psum.28 = f32[2,5]{1,0:T(2,128)S(1)} all-reduce(f32[2,5]{1,0:T(2,128)S(1)} %pad_maximum_fusion), channel_id=1, replica_groups=mesh['dp'=32,'tensor'=4] {'dp','tensor'}, use_global_device_ids=true, to_apply=%region_4.0 | all-reduce | flops 10 | bytes 80 | tf_op jit(solution)/shard_map/psum | solution.py:45
  276.1 0.2 rsqrt_reduce_fusion
  276.2 0.0 copy-done.4
  276.3 0.2 fusion.28
  276.5 0.0 copy-done.8
  276.5 0.0 copy-done.9
  276.5 4.3 %fusion.6 = f32[2,2048]{1,0:T(2,128)S(1)} fusion(f32[2,2048]{1,0:T(2,128)S(1)} %fusion.28, f32[2,512]{1,0:T(2,128)S(1)} %copy-done.9, f32[512,2048]{1,0:T(8,128)} %param.23, f32[2048]{0:T(1024)S(1)} %copy-done.8), kind=kOutput, calls=%fused_computation.8 | convolution fusion | flops 25174016 | bytes 4239360 | tf_op jit(solution)/shard_map/dot_general | solution.py:16
  280.8 0.0 copy-done.10
  280.8 0.0 copy-start.2
  280.8 0.6 divide_multiply_fusion.2
  281.4 0.0 copy-start.7
  281.4 0.0 copy-done
  281.4 0.0 copy-done.15
  281.4 0.2 convolution_add_fusion.1
  281.5 0.3 exponential_reduce_fusion
  281.8 1.4 copy.34
  283.2 0.0 copy-done.12
  283.2 0.0 copy-start.5
  283.2 2.7 fusion.11
  285.9 0.0 copy-start.3
  285.9 0.0 copy-done.6
  285.9 0.0 copy-done.2
  286.0 0.2 broadcast_multiply_fusion
  286.2 0.0 copy-done.7
  286.2 0.4 stack.17
  286.6 0.5 copy.32
  287.1 0.0 copy-start.11
  287.1 0.4 stack.16
  287.5 0.0 copy-done.5
  287.5 0.0 copy-done.3
  287.5 10.4 %stack.18 = f32[2,6,256,256]{3,1,2,0:T(8,128)} concatenate(f32[2,1,256,256]{3,1,2,0:T(1,128)S(1)} %copy.32, f32[2,1,256,256]{3,1,2,0:T(1,128)} %get-tuple-element.35, f32[2,1,256,256]{3,1,2,0:T(1,128)S(1)} %copy-done.3, f32[2,1,256,256]{3,1,2,0:T(1,128)S(1)} %get-tuple-element.33, f32[2,1,256,256]{3,1,2,0:T(1,128)S(1)} %stack.16, f32[2,1,256,256]{3,1,2,0:T(1,128)S(1)} %stack.17), dimensions={1} | concatenate | bytes 6291456 | tf_op jit(solution)/shard_map/stack | solution.py:60
  297.9 0.0 copy-done.11
  297.9 15.3 %fusion.25 = f32[2,256,256,32]{2,3,1,0:T(8,128)S(1)} fusion(f32[2,6,256,256]{3,1,2,0:T(8,128)} %stack.18, f32[6,32]{1,0:T(8,128)S(1)} %copy-done.11), kind=kOutput, calls=%fused_computation.48 | convolution fusion | flops 301989888 | bytes 19923712 | tf_op jit(solution)/shard_map/nh,lnrc->lhrc/dot_general | solution.py:72
  313.2 0.0 copy-done.14
  313.2 9.9 %fusion.8 = f32[2,2,256,256]{3,1,2,0:T(2,128)S(1)} fusion(f32[2,256,256,32]{2,3,1,0:T(8,128)S(1)} %fusion.25, f32[2,32]{1,0:T(2,128)S(1)} %bitcast.58, f32[32,2]{0,1:T(2,128)S(1)} %copy-done.14), kind=kOutput, calls=%fused_computation.12 | convolution fusion | flops 109051904 | bytes 17826304 | tf_op jit(solution)/shard_map/ho,lhrc->lorc/dot_general | solution.py:75
  323.1 0.8 fusion.37
  323.9 1.0 fusion.16
  (6 shorter events, 0.0 us)
Async XLA Ops:
  7.2 274.2 %copy-start = (f32[512,34]{0,1:T(8,128)S(1)}, f32[512,34]{0,1:T(8,128)}, u32[]{:S(2)}) copy-start(f32[512,34]{0,1:T(8,128)} %param.25) | copy-start | bytes 208900
  7.2 127.6 %reduce-scatter.2.cloned.1.call-start = ((), (), s32[]{:S(2)}) async-start(), calls=%async_computation.1 | async-start | bytes 17301504 | tf_op jit(solution)/shard_map/reduce_scatter | solution.py:29
  17.7 1.0 copy-start.1
  17.7 127.3 %copy-start.13 = (f32[2,256]{1,0:T(2,128)S(1)}, f32[2,256]{1,0:T(2,128)}, u32[]{:S(2)}) copy-start(f32[2,256]{1,0:T(2,128)} %param.18) | copy-start | bytes 6148
  17.7 193.3 %copy-start.16 = (f32[3]{0:T(128)S(1)}, f32[3]{0:T(128)}, u32[]{:S(2)}) copy-start(f32[3]{0:T(128)} %constant.35) | copy-start | bytes 40
  17.7 193.3 %copy-start.17 = (f32[3]{0:T(128)S(1)}, f32[3]{0:T(128)}, u32[]{:S(2)}) copy-start(f32[3]{0:T(128)} %constant.32.clone) | copy-start | bytes 40
  18.7 257.5 %copy-start.4 = (f32[5,2048]{1,0:T(8,128)S(1)}, f32[5,2048]{1,0:T(8,128)}, u32[]{:S(2)}) copy-start(f32[5,2048]{1,0:T(8,128)} %param.22) | copy-start | bytes 122884
  18.7 257.8 %copy-start.8 = (f32[2048]{0:T(1024)S(1)}, f32[2048]{0:T(1024)}, u32[]{:S(2)}) copy-start(f32[2048]{0:T(1024)} %param.24) | copy-start | bytes 24580
  18.7 257.8 %copy-start.9 = (f32[2,512]{1,0:T(2,128)S(1)}, f32[2,512]{1,0:T(2,128)}, u32[]{:S(2)}) copy-start(f32[2,512]{1,0:T(2,128)} %param.20) | copy-start | bytes 12292
  145.1 140.9 %copy-start.6 = (f32[2,256]{1,0:T(2,128)}, f32[2,256]{1,0:T(2,128)S(1)}, u32[]{:S(2)}) copy-start(f32[2,256]{1,0:T(2,128)S(1)} %get-tuple-element.32) | copy-start | bytes 6148
  211.0 69.8 %copy-start.10 = (f32[2,512]{1,0:T(2,128)S(1)}, f32[2,512]{1,0:T(2,128)}, u32[]{:S(2)}) copy-start(f32[2,512]{1,0:T(2,128)} %param.21) | copy-start | bytes 12292
  211.0 70.4 %copy-start.15 = (f32[34]{0:T(128)S(1)}, f32[34]{0:T(128)}, u32[]{:S(2)}) copy-start(f32[34]{0:T(128)} %param.26) | copy-start | bytes 412
  214.0 69.2 %copy-start.12 = (f32[2,256]{1,0:T(2,128)S(1)}, f32[2,256]{1,0:T(2,128)}, u32[]{:S(2)}) copy-start(f32[2,256]{1,0:T(2,128)} %param.19) | copy-start | bytes 6148
  280.8 5.2 %copy-start.2 = (f32[2,256,256]{2,1,0:T(8,128)S(1)}, f32[2,256,256]{2,1,0:T(8,128)}, u32[]{:S(2)}) copy-start(f32[2,256,256]{2,1,0:T(8,128)} %reduce-scatter.2.cloned.1.call-done) | copy-start | bytes 1572868
  281.4 4.8 %copy-start.7 = (f32[2,512]{1,0:T(2,128)}, f32[2,512]{1,0:T(2,128)S(1)}, u32[]{:S(2)}) copy-start(f32[2,512]{1,0:T(2,128)S(1)} %get-tuple-element.27) | copy-start | bytes 12292
  283.2 4.2 %copy-start.5 = (f32[2,256]{1,0:T(2,128)}, f32[2,256]{1,0:T(2,128)S(1)}, u32[]{:S(2)}) copy-start(f32[2,256]{1,0:T(2,128)S(1)} %multiply_add_fusion) | copy-start | bytes 6148
  285.9 1.6 copy-start.3
  287.1 10.8 %copy-start.11 = (f32[6,32]{1,0:T(8,128)S(1)}, f32[6,32]{1,0:T(8,128)}, u32[]{:S(2)}) copy-start(f32[6,32]{1,0:T(8,128)} %param.27) | copy-start | bytes 2308
  297.9 15.3 %copy-start.14 = (f32[32,2]{0,1:T(2,128)S(1)}, f32[32,2]{0,1:T(2,128)}, u32[]{:S(2)}) copy-start(f32[32,2]{0,1:T(2,128)} %param.28) | copy-start | bytes 772
Sparse Core Ops, SparseCore 0:
  17.8 116.8 reduce-scatter.1
where the time goes:
time: 333 us; the launch traced here: 332 us
  blocking collectives  137 us (41%)
  waiting for transfers between devices  116 us (35%)
  matrix products  29.8 us (9%)
  other arithmetic  20 us (6%)
  local copies, waits for them, and re-layouts  15.2 us (5%)
  between operations  14.2 us (4%)
    reduce_scatter x1, waiting for transfers between devices, process(): lax.psum_scatter(contrib[0].astype(jnp.float32), 'dp', scatter_dimension=...  116 us
    psum x1, blocking collectives, process(): row_total = lax.psum(jnp.sum(rows_new, 1), 'dp')  65.9 us
    psum x1, blocking collectives, process(): stat_sum = lax.psum(stat_part, ('dp', 'tensor'))  62 us
    dot_general x1, matrix products, process(): jnp.einsum('nh,lnrc->lhrc', mlp_first, inputs, precision=HIGH)  15.3 us
    another operation x4, local copies, waits for them, and re-layouts, process(): jnp.stack([grad * scale, moments_new[0] * scale, moments_new[1] * scale,...  11.6 us
    convert_element_type x1, other arithmetic, process(): contrib[0].astype(jnp.float32)  10.4 us
    dot_general x1, matrix products, process(): jnp.einsum('ho,lhrc->lorc', mlp_second, hidden_units, precision=HIGH)  9.85 us
    psum x1, blocking collectives, process(): row_sum = lax.psum(row_part, 'tensor')  8.88 us
  transfers between devices with their start and end apart: 1, of which 1 were waited for; matrix products, arithmetic and copies ran while one was open for 0% of the time, Pallas kernels for 0%

commit v1 on v0

v1 whole, which is shorter than its diff:
```python
import functools

import jax
import jax.numpy as jnp
import numpy as np
from jax import lax
from jax.experimental import pallas as pl
from jax.experimental.pallas import tpu as pltpu
from jax.sharding import PartitionSpec as P

D = 8192
KV = 1024
L = 2
H = 512
HID = 32
NF = 6
CH = 4
NC = L * CH
RB = 256
CB = 256
RQ = RB // CH // 4
MESH = pl.DeviceIdType.MESH
F32 = jnp.float32
BF16 = jnp.bfloat16
DECAYS = tuple(np.float32(v) for v in (0.5, 0.9, 0.99))


def lane_to_rows(row):
    return jnp.transpose(jnp.broadcast_to(row, (128, 128)))


def rows_to_lane(block):
    return jnp.transpose(block)[0:1, :]


def kernel(
    grads, params, moments, row_stat, col_stat, hidden, cell, input_w, recur_w, gate_bias, head_w, head_bias, w1, w2,
    o_params, o_moms, o_rows, o_cols, o_hid, o_cell,
    graw, stage, acc, r1a, r1b, r2a, r2b,
    v_params, v_moms, v_row, v_col, v_hid, v_cell, v_iw, v_rw, v_gb, v_hw, v_hb, v_w1, v_w2,
    n_params, n_moms, n_rows, n_cols, n_hid, n_cell,
    gsum, rowrep, colacc, macc, pacc, pre, headt, hbcol, wst, w2rep, zs, zr, ps, pr, mod, norms, colrow,
    in_sem, g_sem, out_sem, s_sem, d_rs, r1a_rs, r1b_rs, r2a_rs, r2b_rs, z_ss, z_rs, p_ss, p_rs,
):
    dp = lax.axis_index("dp")
    z = lax.axis_index("tensor")
    x = dp // 8
    y = (dp // 2) % 4
    c = dp % 2

    def dev(dx=0, dy=0, dc=0, dz=0):
        return (((x + dx) % 4) * 8 + ((y + dy) % 4) * 2 + (c + dc) % 2, (z + dz) % 4)

    def send(src, dst, ss, rs, target):
        pltpu.make_async_remote_copy(
            src_ref=src, dst_ref=dst, send_sem=ss, recv_sem=rs, device_id=target, device_id_type=MESH
        ).start()

    def wait_all(ref, sem):
        pltpu.make_async_copy(ref, ref, sem).wait()

    barrier = pltpu.get_barrier_semaphore()

    def greet(i, carry):
        pl.semaphore_signal(barrier, inc=1, device_id=dev(i // 8, (i // 2) % 4, i % 2), device_id_type=MESH)
        return carry

    lax.fori_loop(1, 32, greet, 0)
    for dz in range(1, 4):
        pl.semaphore_signal(barrier, inc=1, device_id=dev(dz=dz), device_id_type=MESH)

    def g_copy(k):
        part = pl.ds((k % CH) * 4 * RQ, 4 * RQ)
        return pltpu.make_async_copy(grads.at[k // CH, :, :, :, part, :], graw.at[k], g_sem.at[k])

    ins = [
        pltpu.make_async_copy(a, b, in_sem.at[i])
        for i, (a, b) in enumerate(
            (
                (params, v_params), (moments, v_moms), (row_stat, v_row), (col_stat, v_col), (hidden, v_hid),
                (cell, v_cell), (input_w, v_iw), (recur_w, v_rw), (gate_bias, v_gb), (head_w, v_hw),
                (head_bias, v_hb), (w1, v_w1), (w2, v_w2),
            )
        )
    ]
    for k in range(NC):
        g_copy(k).start()
    for copy in ins:
        copy.start()

    rows = [pl.ds(q * RQ, RQ) for q in range(4)]

    def spread(k, core, write):
        def step(i, carry):
            a, b = i // 4, i % 4
            for q in range(4):
                v = graw[k, a, b, core, rows[q], :].astype(F32)
                write(q, a if q < 2 else b, b if q < 2 else a, v)
            return carry

        lax.fori_loop(0, 16, step, 0)

    def stage_d(k):
        g_copy(k).wait()

        def write(q, i, j, v):
            stage[k, q, i, j] = v

        spread(k, 1 - c, write)
        if k == 0:
            pl.semaphore_wait(barrier, 34)
        send(stage.at[k], acc.at[k], s_sem.at[0], d_rs.at[k], dev(dc=1))

    first = (x, y)
    second = (y, x)
    ways = ((dev(dx=1), dev(dx=3)), (dev(dy=1), dev(dy=3)))

    def stage_1(k):
        wait_all(acc.at[k], d_rs.at[k])

        def write(q, i, j, v):
            acc[k, q, i, j] += v

        spread(k, c, write)
        for h in range(2):
            i0, (plus, minus), qa, qb = first[h], ways[h], 2 * h, 2 * h + 1
            send(acc.at[k, qa, (i0 + 2) % 4], r1a.at[k, qa], s_sem.at[1], r1a_rs.at[k], plus)
            send(acc.at[k, qb, (i0 + 2) % 4], r1a.at[k, qb], s_sem.at[1], r1a_rs.at[k], minus)
        for h in range(2):
            i0, (plus, minus), qa, qb = first[h], ways[h], 2 * h, 2 * h + 1
            send(acc.at[k, qb, (i0 + 1) % 4], r1b.at[k, qb, 0], s_sem.at[2], r1b_rs.at[k], plus)
            send(acc.at[k, qa, (i0 + 3) % 4], r1b.at[k, qa, 1], s_sem.at[2], r1b_rs.at[k], minus)

    def stage_2(k):
        wait_all(r1a.at[k], r1a_rs.at[k])
        for h in range(2):
            i0, (plus, minus), qa, qb = first[h], ways[h], 2 * h, 2 * h + 1
            acc[k, qa, (i0 + 1) % 4] += r1a[k, qa]
            send(acc.at[k, qa, (i0 + 1) % 4], r1b.at[k, qa, 0], s_sem.at[2], r1b_rs.at[k], plus)
            acc[k, qb, (i0 + 3) % 4] += r1a[k, qb]
            send(acc.at[k, qb, (i0 + 3) % 4], r1b.at[k, qb, 1], s_sem.at[2], r1b_rs.at[k], minus)

    def stage_3(k):
        wait_all(r1b.at[k], r1b_rs.at[k])
        for h in range(2):
            i0, j0, (plus, minus), qa, qb = first[h], second[h], ways[1 - h], 2 * h, 2 * h + 1
            for q in (qa, qb):
                acc[k, q, i0] += r1b[k, q, 0] + r1b[k, q, 1]
            send(acc.at[k, qa, i0, (j0 + 2) % 4], r2a.at[k, qa], s_sem.at[3], r2a_rs.at[k], plus)
            send(acc.at[k, qb, i0, (j0 + 2) % 4], r2a.at[k, qb], s_sem.at[3], r2a_rs.at[k], minus)
            send(acc.at[k, qb, i0, (j0 + 1) % 4], r2b.at[k, qb, 0], s_sem.at[4], r2b_rs.at[k], plus)
            send(acc.at[k, qa, i0, (j0 + 3) % 4], r2b.at[k, qa, 1], s_sem.at[4], r2b_rs.at[k], minus)

    def stage_4(k):
        wait_all(r2a.at[k], r2a_rs.at[k])
        for h in range(2):
            i0, j0, (plus, minus), qa, qb = first[h], second[h], ways[1 - h], 2 * h, 2 * h + 1
            acc[k, qa, i0, (j0 + 1) % 4] += r2a[k, qa]
            send(acc.at[k, qa, i0, (j0 + 1) % 4], r2b.at[k, qa, 0], s_sem.at[4], r2b_rs.at[k], plus)
            acc[k, qb, i0, (j0 + 3) % 4] += r2a[k, qb]
            send(acc.at[k, qb, i0, (j0 + 3) % 4], r2b.at[k, qb, 1], s_sem.at[4], r2b_rs.at[k], minus)

    def stage_5(k):
        l = k // CH
        wait_all(r2b.at[k], r2b_rs.at[k])
        for q in range(4):
            h = q // 2
            span = pl.ds((k % CH) * 4 * RQ + q * RQ, RQ)
            g = acc[k, q, first[h], second[h]] + r2b[k, q, 0] + r2b[k, q, 1]
            gsum[l, span, :] = g
            sq = g * g
            rowrep[l, span, :] = jnp.broadcast_to(jnp.sum(sq, 1, keepdims=True), (RQ, 128))
            colacc[l] += jnp.sum(sq.reshape(RQ // 8, 8, CB), 0)
            for n in range(3):
                m = DECAYS[n] * v_moms[n, l, span, :] + (np.float32(1) - DECAYS[n]) * g
                n_moms[n, l, span, :] = m
                macc[l, n] += jnp.sum((m * m).reshape(RQ // 8, 8, CB), 0)
        if k % CH == CH - 1:
            for n in range(3):
                out_copy(n_moms.at[n, l], o_moms.at[n, l], 3 * l + n).start()

    def out_copy(src, dst, i):
        return pltpu.make_async_copy(src, dst, out_sem.at[i])

    lane = lax.broadcasted_iota(jnp.int32, (1, 128), 1)

    def prepare():
        for copy in ins:
            copy.wait()
        colacc[...] = jnp.zeros_like(colacc)
        macc[...] = jnp.zeros_like(macc)
        for l in range(L):
            def square(i, s):
                v = v_params[l, pl.ds(pl.multiple_of(i * 8, 8), 8), :]
                return s + v * v

            pacc[l] = lax.fori_loop(0, RB // 8, square, jnp.zeros((8, CB), F32))
        reps = [jnp.concatenate([lane_to_rows(v_hid[l:l + 1, i * 128:(i + 1) * 128]) for i in range(4)], 0) for l in range(L)]
        for l in range(L):
            mod[l] = reps[l]

        def recur(i, sums):
            at = pl.ds(pl.multiple_of(i * 8, 8), 8)
            w = v_rw[at, :]
            return tuple(sums[l] + w * jnp.tile(mod[l, at, :], (1, 16)) for l in range(L))

        sums = lax.fori_loop(0, H // 8, recur, tuple(jnp.zeros((8, 4 * H), F32) for _ in range(L)))
        for l in range(L):
            pre[l] = jnp.sum(sums[l], 0, keepdims=True) + v_gb[...]
        for i in range(4):
            part = v_hw[i * 128:(i + 1) * 128, :]
            part = jnp.concatenate([part, jnp.zeros((128, 126 - HID), F32)], 1)
            headt[:, i * 128:(i + 1) * 128] = jnp.transpose(part)[0:40, :]
        hbcol[...] = lane_to_rows(jnp.concatenate([v_hb[...], jnp.zeros((1, 126 - HID), F32)], 1))[0:40, :]
        w1t = jnp.concatenate([v_w1[...], jnp.zeros((128 - NF, HID), F32)], 0)
        w1t = jnp.transpose(jnp.concatenate([w1t, jnp.zeros((128, 128 - HID), F32)], 1))[0:HID, :]
        at = lax.broadcasted_iota(jnp.int32, (HID, 256), 1)
        wide = jnp.zeros((HID, 256), F32)
        for n in range(NF):
            hit = ((at // 8) % NF == n) & (at < 144)
            wide = jnp.where(hit, jnp.broadcast_to(w1t[:, n:n + 1], (HID, 256)), wide)
        tall = jnp.broadcast_to(wide[:, None, :], (HID, 8, 256)).reshape(HID * 8, 256)
        tall_at = lax.broadcasted_iota(jnp.int32, (HID * 8, 256), 1)
        tall_row = lax.broadcasted_iota(jnp.int32, (HID * 8, 256), 0)
        tall = jnp.where(tall_at % 8 == tall_row % 8, tall, 0.0)
        high = tall.astype(BF16).astype(F32)
        wst[...] = jnp.where(tall_at < 96, high, tall - high).astype(BF16)
        for o in range(2):
            w2rep[o] = jnp.broadcast_to(v_w2[:, o:o + 1], (HID, 128))

    def total(v):
        return jnp.sum(jnp.sum(v, 0, keepdims=True), 1, keepdims=True)

    def put(values):
        row = jnp.zeros((1, 128), F32)
        for j, v in enumerate(values):
            row = jnp.where(lane == j, v, row)
        return row

    def pick(row, j):
        return jnp.sum(jnp.where(lane == j, row, 0.0), 1, keepdims=True)

    def z_send(l):
        for i in range(2):
            zs[l, :, i * 128:(i + 1) * 128] = rows_to_lane(rowrep[l, i * 128:(i + 1) * 128, :])
        zs[l, :, 256:384] = put([total(colacc[l]), total(macc[l, 0]), total(macc[l, 1]), total(macc[l, 2]), total(pacc[l])])
        for dz in range(1, 4):
            send(zs.at[l], zr.at[l, dz - 1], z_ss.at[l], z_rs.at[l], dev(dz=dz))

    def p_send(l):
        wait_all(zr.at[l], z_rs.at[l])
        got = zs[l] + zr[l, 0] + zr[l, 1] + zr[l, 2]
        new = 0.9 * v_row[l:l + 1, :] + 0.1 * got[:, 0:256] / KV
        n_rows[l:l + 1, :] = new
        ps[l, :, 0:256] = jnp.sum(colacc[l], 0, keepdims=True)
        ps[l, :, 256:384] = got[:, 256:384] + jnp.where(lane == 5, jnp.sum(new, 1, keepdims=True), 0.0)

        def out(i, carry):
            send(ps.at[l], pr.at[l, i - 1], p_ss.at[l], p_rs.at[l], dev(i // 8, (i // 2) % 4, i % 2))
            return carry

        lax.fori_loop(1, 32, out, 0)
        for i in range(2):
            rowrep[l, i * 128:(i + 1) * 128, :] = lane_to_rows(new[:, i * 128:(i + 1) * 128])

    def control(l):
        wait_all(pr.at[l], p_rs.at[l])
        got = ps[l] + jnp.sum(pr[l], 0)
        new = 0.9 * v_col[l:l + 1, :] + 0.1 * got[:, 0:256] / D
        n_cols[l:l + 1, :] = new
        sums = got[:, 256:384]
        means = sums / (D * KV)
        stats = jnp.log(means + 1e-06)
        gates = pre[l]
        for j in range(5):
            gates = gates + pick(stats, j) * v_iw[j:j + 1, :]
        i_g = jax.nn.sigmoid(gates[:, 0:H])
        f_g = jax.nn.sigmoid(gates[:, H:2 * H])
        c_g = jnp.tanh(gates[:, 2 * H:3 * H])
        o_g = jax.nn.sigmoid(gates[:, 3 * H:])
        new_cell = f_g * v_cell[l:l + 1, :] + i_g * c_g
        new_hid = o_g * jnp.tanh(new_cell)
        n_cell[l:l + 1, :] = new_cell
        n_hid[l:l + 1, :] = new_hid
        m = jnp.sum(headt[...] * new_hid, 1, keepdims=True) + hbcol[...]
        mod[l, 0:40, :] = m
        mod[l, 32:33, :] = jnp.exp(m[32:33, :])
        mod[l, 33:34, :] = 0.5 * m[33:34, :]
        row_mean = pick(sums, 5) / D
        colrow[l] = new / row_mean
        norms[l] = jnp.broadcast_to(
            jnp.where(lane == 0, lax.rsqrt(pick(means, 4) + 1e-06), lax.rsqrt(pick(means, 0) + 1e-06)), (1, 128)
        )

    def network(l, begin, end):
        def step(i, carry):
            at = pl.ds(pl.multiple_of(i * 8, 8), 8)
            g = gsum[l, at, :]
            p = v_params[l, at, :]
            scale = lax.rsqrt(jnp.tile(rowrep[l, at, :], (1, 2)) * colrow[l] + 1e-08)
            p_norm = pick(norms[l], 0)
            g_norm = pick(norms[l], 1)
            ins = jnp.concatenate(
                [g * scale] + [n_moms[n, l, at, :] * scale for n in range(3)] + [p * p_norm, g * g_norm], 0
            )
            high = ins.astype(BF16)
            low = (ins - high.astype(F32)).astype(BF16)
            units = jnp.dot(
                wst[:, 0:144], jnp.concatenate([high, low, high], 0), preferred_element_type=F32
            )
            direction = jnp.zeros((8, CB), F32)
            magnitude = jnp.zeros((8, CB), F32)
            for h in range(HID):
                u = jnp.maximum(units[h * 8:(h + 1) * 8, :] + jnp.tile(mod[l, h:h + 1, :], (1, 2)), 0.0)
                direction = direction + jnp.tile(w2rep[0, h:h + 1, :], (1, 2)) * u
                magnitude = magnitude + jnp.tile(w2rep[1, h:h + 1, :], (1, 2)) * u
            rate = jnp.tile(mod[l, 32:33, :], (1, 2))
            gain = jnp.tile(mod[l, 33:34, :], (1, 2))
            n_params[l, at, :] = p - rate * direction * jnp.exp(gain * magnitude)
            return carry

        lax.fori_loop(begin, end, step, 0)

    stage_d(0)
    stage_d(1)
    for t in range(NC + 4):
        if t < NC:
            stage_1(t)
        if t + 2 < NC:
            stage_d(t + 2)
        if 0 <= t - 1 < NC:
            stage_2(t - 1)
        if t == 1:
            prepare()
        if 0 <= t - 2 < NC:
            stage_3(t - 2)
        if 0 <= t - 3 < NC:
            stage_4(t - 3)
        if 0 <= t - 4 < NC:
            stage_5(t - 4)
        if t == CH + 3:
            z_send(0)
        if t == CH + 4:
            p_send(0)
        if t == CH + 5:
            control(0)
    z_send(1)
    network(0, 0, 16)
    p_send(1)
    network(0, 16, 32)
    outs = [
        out_copy(n_params.at[0], o_params.at[0], 6),
        out_copy(n_params.at[1], o_params.at[1], 7),
        out_copy(n_rows, o_rows, 8),
        out_copy(n_cols, o_cols, 9),
        out_copy(n_hid, o_hid, 10),
        out_copy(n_cell, o_cell, 11),
    ]
    outs[0].start()
    outs[2].start()
    control(1)
    for i in (3, 4, 5):
        outs[i].start()
    network(1, 0, 32)
    outs[1].start()
    for l in range(L):
        for n in range(3):
            out_copy(n_moms.at[n, l], o_moms.at[n, l], 3 * l + n).wait()
    wait_all(acc, s_sem.at[0])
    wait_all(r1a, s_sem.at[1])
    wait_all(r1b, s_sem.at[2])
    wait_all(r2a, s_sem.at[3])
    wait_all(r2b, s_sem.at[4])
    for l in range(L):
        wait_all(zr.at[l], z_ss.at[l])
        wait_all(pr.at[l], p_ss.at[l])
    for copy in outs:
        copy.wait()


def body(grads, params, moments, row_stat, col_stat, hidden, cell, input_w, recur_w, gate_bias, head_w, head_bias, w1, w2):
    any_space = pl.BlockSpec(memory_space=pl.ANY)
    vmem = pltpu.VMEM
    dma = pltpu.SemaphoreType.DMA
    quarter = (RQ, CB)
    return pl.pallas_call(
        kernel,
        out_shape=(
            jax.ShapeDtypeStruct((L, RB, CB), F32),
            jax.ShapeDtypeStruct((3, L, RB, CB), F32),
            jax.ShapeDtypeStruct((L, RB), F32),
            jax.ShapeDtypeStruct((L, CB), F32),
            jax.ShapeDtypeStruct((L, H), F32),
            jax.ShapeDtypeStruct((L, H), F32),
        ),
        in_specs=[any_space] * 14,
        out_specs=(any_space,) * 6,
        scratch_shapes=[
            vmem((NC, 4, 4, 2, 4 * RQ, CB), BF16),
            vmem((NC, 4, 4, 4) + quarter, F32),
            vmem((NC, 4, 4, 4) + quarter, F32),
            vmem((NC, 4, 4) + quarter, F32),
            vmem((NC, 4, 2, 4) + quarter, F32),
            vmem((NC, 4) + quarter, F32),
            vmem((NC, 4, 2) + quarter, F32),
            vmem((L, RB, CB), F32),
            vmem((3, L, RB, CB), F32),
            vmem((L, RB), F32),
            vmem((L, CB), F32),
            vmem((L, H), F32),
            vmem((L, H), F32),
            vmem((5, 4 * H), F32),
            vmem((H, 4 * H), F32),
            vmem((1, 4 * H), F32),
            vmem((H, HID + 2), F32),
            vmem((1, HID + 2), F32),
            vmem((NF, HID), F32),
            vmem((HID, 2), F32),
            vmem((L, RB, CB), F32),
            vmem((3, L, RB, CB), F32),
            vmem((L, RB), F32),
            vmem((L, CB), F32),
            vmem((L, H), F32),
            vmem((L, H), F32),
            vmem((L, RB, CB), F32),
            vmem((L, RB, 128), F32),
            vmem((L, 8, CB), F32),
            vmem((L, 3, 8, CB), F32),
            vmem((L, 8, CB), F32),
            vmem((L, 1, 4 * H), F32),
            vmem((40, H), F32),
            vmem((40, 128), F32),
            vmem((HID * 8, 256), BF16),
            vmem((2, HID, 128), F32),
            vmem((L, 1, 384), F32),
            vmem((L, 3, 1, 384), F32),
            vmem((L, 1, 384), F32),
            vmem((L, 31, 1, 384), F32),
            vmem((L, H, 128), F32),
            vmem((L, 1, 128), F32),
            vmem((L, 1, CB), F32),
            dma((13,)),
            dma((NC,)),
            dma((12,)),
            dma((5,)),
            dma((NC,)),
            dma((NC,)),
            dma((NC,)),
            dma((NC,)),
            dma((NC,)),
            dma((L,)),
            dma((L,)),
            dma((L,)),
            dma((L,)),
        ],
        compiler_params=pltpu.CompilerParams(
            collective_id=0, has_side_effects=True, vmem_limit_bytes=60 * 2**20
        ),
        name="update",
    )(
        grads.reshape(L, 4, 4, 2, RB, CB), params, moments, row_stat, col_stat, hidden, cell, input_w, recur_w,
        gate_bias.reshape(1, 4 * H), head_w, head_bias.reshape(1, HID + 2), w1, w2,
    )


def solution(mesh):
    return jax.shard_map(
        body,
        mesh=mesh,
        in_specs=(
            P("dp", None, None, "tensor"),
            P(None, "dp", "tensor"),
            P(None, None, "dp", "tensor"),
            P(None, "dp"),
            P(None, "tensor"),
        )
        + (P(),) * 9,
        out_specs=(
            P(None, "dp", "tensor"),
            P(None, None, "dp", "tensor"),
            P(None, "dp"),
            P(None, "tensor"),
            P(),
            P(),
        ),
        check_vma=False,
    )
```

time: 333 us -> 92.4 us (0.28)
  blocking collectives: 137 us -> 0 us
  waiting for transfers between devices: 116 us -> 0 us
  Pallas kernels: 0 us -> 81.5 us
  matrix products: 29.8 us -> 0 us
  other arithmetic: 20 us -> 0 us
  between operations: 14.2 us -> 0.65 us
  local copies, waits for them, and re-layouts: 15.2 us -> 10.1 us
    psum x3 -> x0, blocking collectives: 137 us -> none  [the longest x1 65.9 us: process(): row_total = lax.psum(jnp.sum(rows_new, 1), 'dp')]
    reduce_scatter x1 -> x0, waiting for transfers between devices: 116 us -> none  [process(): lax.psum_scatter(contrib[0].astype(jnp.float32), 'dp', scatter_dimension=...]
    pallas_call x0 -> x1, Pallas kernels: none -> 81.5 us  [body(): pl.pallas_call(kernel, out_shape=(jax.ShapeDtypeStruct((L, RB, CB), F32),...]
    dot_general x5 -> x0, matrix products: 29.8 us -> none  [the longest x1 15.3 us: process(): jnp.einsum('nh,lnrc->lhrc', mlp_first, inputs, precision=HIGH)]
    another operation x4 -> x0, local copies, waits for them, and re-layouts: 11.6 us -> none  [process(): jnp.stack([grad * scale, moments_new[0] * scale, moments_new[1] * scale,...]
    convert_element_type x1 -> x0, other arithmetic: 10.4 us -> none  [process(): contrib[0].astype(jnp.float32)]
    unnamed x37 -> x16, local copies, waits for them, and re-layouts: 2.52 us -> 10.1 us
    reduce_sum x4 -> x0, other arithmetic: 4.53 us -> none  [the longest x1 3 us: process(): jnp.sum(moments_new * moments_new, (2, 3))]
  transfers between devices with their start and end apart: 1 -> 0, of which waited for: 1 -> 0; matrix products, arithmetic and copies ran while one was open for 0% -> 0% of each run, Pallas kernels for 0% -> 0%
where the time goes in v1:
time: 92.4 us; the launch traced here: 92.2 us
  Pallas kernels  81.5 us (88%)
  local copies, waits for them, and re-layouts  10.1 us (11%)
    pallas_call x1, Pallas kernels, body(): pl.pallas_call(kernel, out_shape=(jax.ShapeDtypeStruct((L, RB, CB), F32),...  81.5 us
    unnamed x16, local copies, waits for them, and re-layouts  10.1 us

profile of v1, /device:TPU:1, one launch (start us, length us, event | category | flops | bytes accessed | tf_op | source)
XLA Modules:
  0.0 92.2 jit_solution(2726723407180062745)
XLA Ops:
  0.6 1.4 %copy.21.w2 = f32[32,2]{1,0:T(8,128)} copy(f32[32,2]{0,1:T(2,128)} %param.27) | data formatting | bytes 512 | tf_op args[13]
  2.0 1.7 %copy.20.head_w = f32[512,34]{1,0:T(8,128)} copy(f32[512,34]{0,1:T(8,128)} %param.24) | data formatting | bytes 139264 | tf_op args[10]
  3.7 81.5 %update.1 = (f32[2,256,256]{2,1,0:T(8,128)}, f32[3,2,256,256]{3,2,1,0:T(8,128)}, f32[2,256]{1,0:T(2,128)}, f32[2,256]{1,0:T(2,128)}, f32[2,512]{1,0:T(2,128)}, /*index=5*/f32[2,512]{1,0:T(2,128)}) custom-call(bf16[2,4,4,2,256,256]{5,4,3,2,1,0:T(8,128)(2,1)} %bitcast.3, f32[2,256,256]{2,1,0:T(8,128)} %params.1, f32[3,2,256,256]{3,2,1,0:T(8,128)} %moments.1, ...), custom_call_target="tpu_custom_call" | custom-call | tf_op jit(solution)/shard_map/update/pallas_call | solution.py:386
  85.2 1.9 %copy.28 = f32[2,256,256]{2,1,0:T(8,128)} copy(f32[2,256,256]{2,1,0:T(8,128)} %get-tuple-element.12) | data formatting | bytes 1048576
  87.1 0.0 copy-start.3
  87.1 0.0 copy-start.2
  87.1 0.0 copy-start.1
  87.1 0.0 copy-start
  87.1 2.7 %copy.29 = f32[3,2,256,256]{3,2,1,0:T(8,128)} copy(f32[3,2,256,256]{3,2,1,0:T(8,128)} %get-tuple-element.13) | data formatting | bytes 3145728
  89.8 0.0 copy-done.3
  89.8 0.6 copy.30
  90.4 0.0 copy-done.2
  90.4 0.6 copy.31
  91.0 0.0 copy-done.1
  91.0 0.6 copy.32
  91.6 0.0 copy-done
  91.6 0.6 copy.33
Async XLA Ops:
  87.1 2.8 %copy-start.3 = (f32[2,256]{1,0:T(2,128)S(1)}, f32[2,256]{1,0:T(2,128)}, u32[]{:S(2)}) copy-start(f32[2,256]{1,0:T(2,128)} %get-tuple-element.14) | copy-start | bytes 6148
  87.1 3.3 %copy-start.2 = (f32[2,256]{1,0:T(2,128)S(1)}, f32[2,256]{1,0:T(2,128)}, u32[]{:S(2)}) copy-start(f32[2,256]{1,0:T(2,128)} %get-tuple-element.15) | copy-start | bytes 6148
  87.1 3.9 %copy-start.1 = (f32[2,512]{1,0:T(2,128)S(1)}, f32[2,512]{1,0:T(2,128)}, u32[]{:S(2)}) copy-start(f32[2,512]{1,0:T(2,128)} %get-tuple-element.16) | copy-start | bytes 12292
  87.1 4.5 %copy-start = (f32[2,512]{1,0:T(2,128)S(1)}, f32[2,512]{1,0:T(2,128)}, u32[]{:S(2)}) copy-start(f32[2,512]{1,0:T(2,128)} %get-tuple-element.17) | copy-start | bytes 12292

commit v2 on v1

--- a/solution.py
+++ b/solution.py
@@ -14,6 +14,7 @@
 H = 512
 HID = 32
 NF = 6
+AHEAD = 2
 CH = 4
 NC = L * CH
 RB = 256
@@ -33,14 +34,50 @@
     return jnp.transpose(block)[0:1, :]
 
 
+def twice(v):
+    return jnp.concatenate([v, v], 1)
+
+
+def network(begin, end, g_ref, m_refs, p_ref, row_ref, col_ref, norm_ref, wst_ref, w2_ref, mod_ref, out_ref):
+    ones = jnp.where(lax.broadcasted_iota(jnp.int32, (16, CB), 0) < 2, 1.0, 0.0).astype(BF16)
+
+    def tile(at):
+        g = g_ref[at, :]
+        p = p_ref[at, :]
+        scale = lax.rsqrt(twice(row_ref[at, :]) * col_ref[...] + 1e-08)
+        ins = [g * scale] + [m[at, :] * scale for m in m_refs]
+        ins += [p * twice(norm_ref[0:1, :]), g * twice(norm_ref[1:2, :])]
+        ins = jnp.concatenate(ins, 0)
+        high = ins.astype(BF16)
+        low = (ins - high.astype(F32)).astype(BF16)
+        units = jnp.dot(
+            wst_ref[:, 0:160], jnp.concatenate([high, low, high, ones], 0), preferred_element_type=F32
+        )
+        direction = jnp.zeros((8, CB), F32)
+        magnitude = jnp.zeros((8, CB), F32)
+        for h in range(HID):
+            u = jnp.maximum(units[h * 8:(h + 1) * 8, :], 0.0)
+            direction = direction + twice(w2_ref[0, h:h + 1, :]) * u
+            magnitude = magnitude + twice(w2_ref[1, h:h + 1, :]) * u
+        rate = twice(mod_ref[HID:HID + 1, :])
+        gain = twice(mod_ref[HID + 1:HID + 2, :])
+        out_ref[at, :] = p - rate * direction * jnp.exp(gain * magnitude)
+
+    def step(i, carry):
+        for u in range(8):
+            tile(pl.ds(pl.multiple_of(i * 64 + u * 8, 8), 8))
+        return carry
+
+    lax.fori_loop(begin, end, step, 0)
+
+
 def kernel(
     grads, params, moments, row_stat, col_stat, hidden, cell, input_w, recur_w, gate_bias, head_w, head_bias, w1, w2,
-    o_params, o_moms, o_rows, o_cols, o_hid, o_cell,
+    n_params, n_moms, v_params, gsum, rowrep, colrow, norms, wst, w2rep, mod, n_rows, n_cols, n_hid, n_cell,
     graw, stage, acc, r1a, r1b, r2a, r2b,
-    v_params, v_moms, v_row, v_col, v_hid, v_cell, v_iw, v_rw, v_gb, v_hw, v_hb, v_w1, v_w2,
-    n_params, n_moms, n_rows, n_cols, n_hid, n_cell,
-    gsum, rowrep, colacc, macc, pacc, pre, headt, hbcol, wst, w2rep, zs, zr, ps, pr, mod, norms, colrow,
-    in_sem, g_sem, out_sem, s_sem, d_rs, r1a_rs, r1b_rs, r2a_rs, r2b_rs, z_ss, z_rs, p_ss, p_rs,
+    v_moms, v_row, v_col, v_hid, v_cell, v_iw, v_rw, v_gb, headt, v_hb, v_w1, v_w2,
+    hidrep, colacc, macc, pacc, pre, hbcol, zs, zr, ps, pr,
+    in_sem, g_sem, s_sem, d_rs, r1a_rs, r1b_rs, r2a_rs, r2b_rs, z_ss, z_rs, p_ss, p_rs,
 ):
     dp = lax.axis_index("dp")
     z = lax.axis_index("tensor")
@@ -59,6 +96,12 @@
     def wait_all(ref, sem):
         pltpu.make_async_copy(ref, ref, sem).wait()
 
+    def g_copy(k):
+        part = pl.ds((k % CH) * 4 * RQ, 4 * RQ)
+        return pltpu.make_async_copy(grads.at[k // CH, :, :, :, part, :], graw.at[k], g_sem.at[k])
+
+    for k in range(AHEAD):
+        g_copy(k).start()
     barrier = pltpu.get_barrier_semaphore()
 
     def greet(i, carry):
@@ -68,40 +111,37 @@
     lax.fori_loop(1, 32, greet, 0)
     for dz in range(1, 4):
         pl.semaphore_signal(barrier, inc=1, device_id=dev(dz=dz), device_id_type=MESH)
-
-    def g_copy(k):
-        part = pl.ds((k % CH) * 4 * RQ, 4 * RQ)
-        return pltpu.make_async_copy(grads.at[k // CH, :, :, :, part, :], graw.at[k], g_sem.at[k])
 
     ins = [
         pltpu.make_async_copy(a, b, in_sem.at[i])
         for i, (a, b) in enumerate(
             (
                 (params, v_params), (moments, v_moms), (row_stat, v_row), (col_stat, v_col), (hidden, v_hid),
-                (cell, v_cell), (input_w, v_iw), (recur_w, v_rw), (gate_bias, v_gb), (head_w, v_hw),
+                (cell, v_cell), (input_w, v_iw), (recur_w, v_rw), (gate_bias, v_gb), (head_w, headt),
                 (head_bias, v_hb), (w1, v_w1), (w2, v_w2),
             )
         )
     ]
-    for k in range(NC):
-        g_copy(k).start()
-    for copy in ins:
-        copy.start()
-
-    rows = [pl.ds(q * RQ, RQ) for q in range(4)]
+    def load_more(k):
+        if k + AHEAD < NC:
+            g_copy(k + AHEAD).start()
+        if k == 1:
+            for copy in ins:
+                copy.start()
 
     def spread(k, core, write):
         def step(i, carry):
             a, b = i // 4, i % 4
+            v = graw[k, a, b, core].astype(F32)
             for q in range(4):
-                v = graw[k, a, b, core, rows[q], :].astype(F32)
-                write(q, a if q < 2 else b, b if q < 2 else a, v)
+                write(q, a if q < 2 else b, b if q < 2 else a, v[q * RQ:(q + 1) * RQ, :])
             return carry
 
         lax.fori_loop(0, 16, step, 0)
 
     def stage_d(k):
         g_copy(k).wait()
+        load_more(k)
 
         def write(q, i, j, v):
             stage[k, q, i, j] = v
@@ -175,12 +215,6 @@
                 m = DECAYS[n] * v_moms[n, l, span, :] + (np.float32(1) - DECAYS[n]) * g
                 n_moms[n, l, span, :] = m
                 macc[l, n] += jnp.sum((m * m).reshape(RQ // 8, 8, CB), 0)
-        if k % CH == CH - 1:
-            for n in range(3):
-                out_copy(n_moms.at[n, l], o_moms.at[n, l], 3 * l + n).start()
-
-    def out_copy(src, dst, i):
-        return pltpu.make_async_copy(src, dst, out_sem.at[i])
 
     lane = lax.broadcasted_iota(jnp.int32, (1, 128), 1)
 
@@ -197,21 +231,17 @@
             pacc[l] = lax.fori_loop(0, RB // 8, square, jnp.zeros((8, CB), F32))
         reps = [jnp.concatenate([lane_to_rows(v_hid[l:l + 1, i * 128:(i + 1) * 128]) for i in range(4)], 0) for l in range(L)]
         for l in range(L):
-            mod[l] = reps[l]
+            hidrep[l] = reps[l]
 
         def recur(i, sums):
             at = pl.ds(pl.multiple_of(i * 8, 8), 8)
             w = v_rw[at, :]
-            return tuple(sums[l] + w * jnp.tile(mod[l, at, :], (1, 16)) for l in range(L))
+            return tuple(sums[l] + w * jnp.tile(hidrep[l, at, :], (1, 16)) for l in range(L))
 
         sums = lax.fori_loop(0, H // 8, recur, tuple(jnp.zeros((8, 4 * H), F32) for _ in range(L)))
         for l in range(L):
             pre[l] = jnp.sum(sums[l], 0, keepdims=True) + v_gb[...]
-        for i in range(4):
-            part = v_hw[i * 128:(i + 1) * 128, :]
-            part = jnp.concatenate([part, jnp.zeros((128, 126 - HID), F32)], 1)
-            headt[:, i * 128:(i + 1) * 128] = jnp.transpose(part)[0:40, :]
-        hbcol[...] = lane_to_rows(jnp.concatenate([v_hb[...], jnp.zeros((1, 126 - HID), F32)], 1))[0:40, :]
+        hbcol[...] = lane_to_rows(jnp.concatenate([v_hb[...], jnp.zeros((1, 126 - HID), F32)], 1))[0:HID + 2, :]
         w1t = jnp.concatenate([v_w1[...], jnp.zeros((128 - NF, HID), F32)], 0)
         w1t = jnp.transpose(jnp.concatenate([w1t, jnp.zeros((128, 128 - HID), F32)], 1))[0:HID, :]
         at = lax.broadcasted_iota(jnp.int32, (HID, 256), 1)
@@ -224,9 +254,12 @@
         tall_row = lax.broadcasted_iota(jnp.int32, (HID * 8, 256), 0)
         tall = jnp.where(tall_at % 8 == tall_row % 8, tall, 0.0)
         high = tall.astype(BF16).astype(F32)
-        wst[...] = jnp.where(tall_at < 96, high, tall - high).astype(BF16)
+        tall = jnp.where(tall_at < 96, high, tall - high).astype(BF16)
+        for l in range(L):
+            wst[l] = tall
         for o in range(2):
-            w2rep[o] = jnp.broadcast_to(v_w2[:, o:o + 1], (HID, 128))
+            row = jnp.concatenate([v_w2[o:o + 1, :], jnp.zeros((1, 128 - HID), F32)], 1)
+            w2rep[o] = lane_to_rows(row)[0:HID, :]
 
     def total(v):
         return jnp.sum(jnp.sum(v, 0, keepdims=True), 1, keepdims=True)
@@ -283,43 +316,24 @@
         n_cell[l:l + 1, :] = new_cell
         n_hid[l:l + 1, :] = new_hid
         m = jnp.sum(headt[...] * new_hid, 1, keepdims=True) + hbcol[...]
-        mod[l, 0:40, :] = m
-        mod[l, 32:33, :] = jnp.exp(m[32:33, :])
-        mod[l, 33:34, :] = 0.5 * m[33:34, :]
+        mod[l, 0:HID + 2, :] = jnp.broadcast_to(m, (HID + 2, 128))
+        mod[l, HID:HID + 1, :] = jnp.broadcast_to(jnp.exp(m[HID:HID + 1, :]), (1, 128))
+        mod[l, HID + 1:HID + 2, :] = jnp.broadcast_to(0.5 * m[HID + 1:HID + 2, :], (1, 128))
+        bias = jnp.broadcast_to(m[0:HID, None, :], (HID, 8, 128)).reshape(HID * 8, 128)
+        high = bias.astype(BF16).astype(F32)
+        side = wst[l, :, 128:256].astype(F32)
+        side = jnp.where(lane == 16, high, jnp.where(lane == 17, bias - high, side))
+        wst[l, :, 128:256] = side.astype(BF16)
         row_mean = pick(sums, 5) / D
         colrow[l] = new / row_mean
-        norms[l] = jnp.broadcast_to(
-            jnp.where(lane == 0, lax.rsqrt(pick(means, 4) + 1e-06), lax.rsqrt(pick(means, 0) + 1e-06)), (1, 128)
+        norms[l, 0:1, :] = jnp.broadcast_to(lax.rsqrt(pick(means, 4) + 1e-06), (1, 128))
+        norms[l, 1:2, :] = jnp.broadcast_to(lax.rsqrt(pick(means, 0) + 1e-06), (1, 128))
+
+    def network_0(begin, end):
+        network(
+            begin, end, gsum.at[0], [n_moms.at[n, 0] for n in range(3)], v_params.at[0], rowrep.at[0], colrow.at[0],
+            norms.at[0], wst.at[0], w2rep, mod.at[0], n_params,
         )
-
-    def network(l, begin, end):
-        def step(i, carry):
-            at = pl.ds(pl.multiple_of(i * 8, 8), 8)
-            g = gsum[l, at, :]
-            p = v_params[l, at, :]
-            scale = lax.rsqrt(jnp.tile(rowrep[l, at, :], (1, 2)) * colrow[l] + 1e-08)
-            p_norm = pick(norms[l], 0)
-            g_norm = pick(norms[l], 1)
-            ins = jnp.concatenate(
-                [g * scale] + [n_moms[n, l, at, :] * scale for n in range(3)] + [p * p_norm, g * g_norm], 0
-            )
-            high = ins.astype(BF16)
-            low = (ins - high.astype(F32)).astype(BF16)
-            units = jnp.dot(
-                wst[:, 0:144], jnp.concatenate([high, low, high], 0), preferred_element_type=F32
-            )
-            direction = jnp.zeros((8, CB), F32)
-            magnitude = jnp.zeros((8, CB), F32)
-            for h in range(HID):
-                u = jnp.maximum(units[h * 8:(h + 1) * 8, :] + jnp.tile(mod[l, h:h + 1, :], (1, 2)), 0.0)
-                direction = direction + jnp.tile(w2rep[0, h:h + 1, :], (1, 2)) * u
-                magnitude = magnitude + jnp.tile(w2rep[1, h:h + 1, :], (1, 2)) * u
-            rate = jnp.tile(mod[l, 32:33, :], (1, 2))
-            gain = jnp.tile(mod[l, 33:34, :], (1, 2))
-            n_params[l, at, :] = p - rate * direction * jnp.exp(gain * magnitude)
-            return carry
-
-        lax.fori_loop(begin, end, step, 0)
 
     stage_d(0)
     stage_d(1)
@@ -345,27 +359,10 @@
         if t == CH + 5:
             control(0)
     z_send(1)
-    network(0, 0, 16)
+    network_0(0, 2)
     p_send(1)
-    network(0, 16, 32)
-    outs = [
-        out_copy(n_params.at[0], o_params.at[0], 6),
-        out_copy(n_params.at[1], o_params.at[1], 7),
-        out_copy(n_rows, o_rows, 8),
-        out_copy(n_cols, o_cols, 9),
-        out_copy(n_hid, o_hid, 10),
-        out_copy(n_cell, o_cell, 11),
-    ]
-    outs[0].start()
-    outs[2].start()
+    network_0(2, 4)
     control(1)
-    for i in (3, 4, 5):
-        outs[i].start()
-    network(1, 0, 32)
-    outs[1].start()
-    for l in range(L):
-        for n in range(3):
-            out_copy(n_moms.at[n, l], o_moms.at[n, l], 3 * l + n).wait()
     wait_all(acc, s_sem.at[0])
     wait_all(r1a, s_sem.at[1])
     wait_all(r1b, s_sem.at[2])
@@ -374,27 +371,64 @@
     for l in range(L):
         wait_all(zr.at[l], z_ss.at[l])
         wait_all(pr.at[l], p_ss.at[l])
-    for copy in outs:
+
+
+def finish(
+    params_0, moms, params, gsum, rowrep, colrow, norms, wst, w2rep, mod, rows, cols, hid, cell,
+    o_params, o_moms, o_rows, o_cols, o_hid, o_cell, params_1, sem,
+):
+    copies = [
+        pltpu.make_async_copy(a, b, sem.at[i])
+        for i, (a, b) in enumerate(
+            ((moms, o_moms), (params_0, o_params.at[0]), (rows, o_rows), (cols, o_cols), (hid, o_hid), (cell, o_cell))
+        )
+    ]
+    for copy in copies:
+        copy.start()
+    for part in range(2):
+        network(
+            2 * part, 2 * part + 2, gsum.at[1], [moms.at[n, 1] for n in range(3)], params.at[1], rowrep.at[1],
+            colrow.at[1], norms.at[1], wst.at[1], w2rep, mod.at[1], params_1,
+        )
+        half = pl.ds(part * RB // 2, RB // 2)
+        copy = pltpu.make_async_copy(params_1.at[half, :], o_params.at[1, half, :], sem.at[6 + part])
+        copy.start()
+        copies.append(copy)
+    for copy in copies:
         copy.wait()
 
 
 def body(grads, params, moments, row_stat, col_stat, hidden, cell, input_w, recur_w, gate_bias, head_w, head_bias, w1, w2):
-    any_space = pl.BlockSpec(memory_space=pl.ANY)
+    hbm = pl.BlockSpec(memory_space=pltpu.HBM)
+    held = pl.BlockSpec(memory_space=pltpu.VMEM)
     vmem = pltpu.VMEM
     dma = pltpu.SemaphoreType.DMA
     quarter = (RQ, CB)
-    return pl.pallas_call(
+    between = (
+        vmem((RB, CB), F32),
+        vmem((3, L, RB, CB), F32),
+        vmem((L, RB, CB), F32),
+        vmem((L, RB, CB), F32),
+        vmem((L, RB, 128), F32),
+        vmem((L, 1, CB), F32),
+        vmem((L, 2, 128), F32),
+        vmem((L, HID * 8, 256), BF16),
+        vmem((2, HID, 128), F32),
+        vmem((L, HID + 2, 128), F32),
+        vmem((L, RB), F32),
+        vmem((L, CB), F32),
+        vmem((L, H), F32),
+        vmem((L, H), F32),
+    )
+    operands = (
+        grads.reshape(L, 4, 4, 2, RB, CB), params, moments, row_stat, col_stat, hidden, cell, input_w, recur_w,
+        gate_bias.reshape(1, 4 * H), head_w.T, head_bias.reshape(1, HID + 2), w1, w2.T,
+    )
+    results = pl.pallas_call(
         kernel,
-        out_shape=(
-            jax.ShapeDtypeStruct((L, RB, CB), F32),
-            jax.ShapeDtypeStruct((3, L, RB, CB), F32),
-            jax.ShapeDtypeStruct((L, RB), F32),
-            jax.ShapeDtypeStruct((L, CB), F32),
-            jax.ShapeDtypeStruct((L, H), F32),
-            jax.ShapeDtypeStruct((L, H), F32),
-        ),
-        in_specs=[any_space] * 14,
-        out_specs=(any_space,) * 6,
+        out_shape=between,
+        in_specs=[hbm] * 14,
+        out_specs=(held,) * len(between),
         scratch_shapes=[
             vmem((NC, 4, 4, 2, 4 * RQ, CB), BF16),
             vmem((NC, 4, 4, 4) + quarter, F32),
@@ -403,7 +437,6 @@
             vmem((NC, 4, 2, 4) + quarter, F32),
             vmem((NC, 4) + quarter, F32),
             vmem((NC, 4, 2) + quarter, F32),
-            vmem((L, RB, CB), F32),
             vmem((3, L, RB, CB), F32),
             vmem((L, RB), F32),
             vmem((L, CB), F32),
@@ -412,36 +445,22 @@
             vmem((5, 4 * H), F32),
             vmem((H, 4 * H), F32),
             vmem((1, 4 * H), F32),
-            vmem((H, HID + 2), F32),
+            vmem((HID + 2, H), F32),
             vmem((1, HID + 2), F32),
             vmem((NF, HID), F32),
-            vmem((HID, 2), F32),
-            vmem((L, RB, CB), F32),
-            vmem((3, L, RB, CB), F32),
-            vmem((L, RB), F32),
-            vmem((L, CB), F32),
-            vmem((L, H), F32),
-            vmem((L, H), F32),
-            vmem((L, RB, CB), F32),
-            vmem((L, RB, 128), F32),
+            vmem((2, HID), F32),
+            vmem((L, H, 128), F32),
             vmem((L, 8, CB), F32),
             vmem((L, 3, 8, CB), F32),
             vmem((L, 8, CB), F32),
             vmem((L, 1, 4 * H), F32),
-            vmem((40, H), F32),
-            vmem((40, 128), F32),
-            vmem((HID * 8, 256), BF16),
-            vmem((2, HID, 128), F32),
+            vmem((HID + 2, 128), F32),
             vmem((L, 1, 384), F32),
             vmem((L, 3, 1, 384), F32),
             vmem((L, 1, 384), F32),
             vmem((L, 31, 1, 384), F32),
-            vmem((L, H, 128), F32),
-            vmem((L, 1, 128), F32),
-            vmem((L, 1, CB), F32),
             dma((13,)),
             dma((NC,)),
-            dma((12,)),
             dma((5,)),
             dma((NC,)),
             dma((NC,)),
@@ -454,13 +473,26 @@
             dma((L,)),
         ],
         compiler_params=pltpu.CompilerParams(
-            collective_id=0, has_side_effects=True, vmem_limit_bytes=60 * 2**20
+            collective_id=0, has_side_effects=True, vmem_limit_bytes=46 * 2**20
         ),
         name="update",
-    )(
-        grads.reshape(L, 4, 4, 2, RB, CB), params, moments, row_stat, col_stat, hidden, cell, input_w, recur_w,
-        gate_bias.reshape(1, 4 * H), head_w, head_bias.reshape(1, HID + 2), w1, w2,
-    )
+    )(*[pltpu.with_memory_space_constraint(v, pltpu.HBM) for v in operands])
+    return pl.pallas_call(
+        finish,
+        out_shape=(
+            jax.ShapeDtypeStruct((L, RB, CB), F32),
+            jax.ShapeDtypeStruct((3, L, RB, CB), F32),
+            jax.ShapeDtypeStruct((L, RB), F32),
+            jax.ShapeDtypeStruct((L, CB), F32),
+            jax.ShapeDtypeStruct((L, H), F32),
+            jax.ShapeDtypeStruct((L, H), F32),
+        ),
+        in_specs=[held] * len(between),
+        out_specs=(hbm,) * 6,
+        scratch_shapes=[vmem((RB, CB), F32), dma((8,))],
+        compiler_params=pltpu.CompilerParams(vmem_limit_bytes=16 * 2**20),
+        name="finish",
+    )(*results)
 
 
 def solution(mesh):

time: 92.4 us -> 75.9 us (0.82)
  local copies, waits for them, and re-layouts: 10.1 us -> 0 us
  Pallas kernels: 81.5 us -> 75.1 us
    unnamed x16 -> x0, local copies, waits for them, and re-layouts: 10.1 us -> none
    pallas_call x1 -> x2, Pallas kernels: 81.5 us -> 75.1 us  [the longest x1 72.2 us: body(): pl.pallas_call(kernel, out_shape=between, in_specs=[hbm] * 14, out_specs=...]
where the time goes in v2:
time: 75.9 us; the launch traced here: 75.7 us
  Pallas kernels  75.1 us (99%)
    pallas_call x1, Pallas kernels, body(): pl.pallas_call(kernel, out_shape=between, in_specs=[hbm] * 14, out_specs=...  72.2 us
    pallas_call x1, Pallas kernels, body(): pl.pallas_call(finish, out_shape=(jax.ShapeDtypeStruct((L, RB, CB), F32),...  2.91 us

profile of v2, /device:TPU:1, one launch (start us, length us, event | category | flops | bytes accessed | tf_op | source)
XLA Modules:
  0.0 75.7 jit_solution(11467941429491877900)
XLA Ops:
  0.6 72.2 %update.1 = (f32[256,256]{1,0:T(8,128)S(1)}, f32[3,2,256,256]{3,2,1,0:T(8,128)S(1)}, f32[2,256,256]{2,1,0:T(8,128)S(1)}, f32[2,256,256]{2,1,0:T(8,128)S(1)}, f32...) custom-call(bf16[2,4,4,2,256,256]{5,4,3,2,1,0:T(8,128)(2,1)} %bitcas, ...), custom_call_target="tpu_custom_call" | custom-call | tf_op jit(solution)/shard_map/update/pallas_call | solution.py:427
  72.8 2.9 %finish.1 = (f32[2,256,256]{2,1,0:T(8,128)}, f32[3,2,256,256]{3,2,1,0:T(8,128)}, f32[2,256]{1,0:T(2,128)}, f32[2,256]{1,0:T(2,128)}, f32[2,512]{1,0:T(2,128)}, /*index=5*/f32[2,512]{1,0:T(2,128)}) custom-call(f32[256,256]{1,0:T(8,128)S(1)} %get-tuple-element.20.params_0, f32[3,2,256,256]{3,2,1,0:T(8,128)S(1)} %get-tuple-element.21.moms, ...), custom_call_target="tpu_custom_call" | custom-call | tf_op jit(solution)/shard_map/finish/pallas_call | solution.py:480

commit v3 on v2

--- a/solution.py
+++ b/solution.py
@@ -15,11 +15,22 @@
 HID = 32
 NF = 6
 AHEAD = 2
-CH = 4
-NC = L * CH
 RB = 256
 CB = 256
-RQ = RB // CH // 4
+RQ = 8
+UR = 4 * RQ
+UT = RB // UR
+NU = L * UT
+SIZES = (1, 2, 2, 3, 3, 2, 2, 1)
+NC = len(SIZES)
+STARTS = tuple(sum(SIZES[:k]) for k in range(NC))
+HALF = STARTS.index(UT)
+ORDER = (
+    (0, 0), (0, 1), (0, 2), (1, 0), (1, 1), (1, 2), (2, 0), (0, 3), (2, 1), (0, 4), (1, 3), (3, 1), (2, 2), (0, 5),
+    (2, 3), (0, 6), (1, 4), (0, 7), (3, 0), ("p", 0), (3, 2), (4, 1), (3, 3), (1, 5), (4, 0), (1, 7), (4, 3), (4, 2),
+    (1, 6), (2, 4), (5, 0), (2, 5), (5, 1), (5, 2), (5, 3), ("x", 0), (2, 6), (2, 7), ("a", 0), (3, 4), (3, 5),
+    (3, 6), (3, 7), (4, 4), (4, 5), (4, 6), (4, 7), ("c", 0), (5, 4), (5, 5), (5, 6), (5, 7),
+)
 MESH = pl.DeviceIdType.MESH
 F32 = jnp.float32
 BF16 = jnp.bfloat16
@@ -76,8 +87,8 @@
     n_params, n_moms, v_params, gsum, rowrep, colrow, norms, wst, w2rep, mod, n_rows, n_cols, n_hid, n_cell,
     graw, stage, acc, r1a, r1b, r2a, r2b,
     v_moms, v_row, v_col, v_hid, v_cell, v_iw, v_rw, v_gb, headt, v_hb, v_w1, v_w2,
-    hidrep, colacc, macc, pacc, pre, hbcol, zs, zr, ps, pr,
-    in_sem, g_sem, s_sem, d_rs, r1a_rs, r1b_rs, r2a_rs, r2b_rs, z_ss, z_rs, p_ss, p_rs,
+    hidrep, colacc, macc, pacc, pre, hbcol, pa, cr, pb, zb, zr, pr, sr,
+    in_sem, g_sem, s_sem, d_rs, r1a_rs, r1b_rs, r2a_rs, r2b_rs, c_ss, c_rs, z_ss, z_rs, p_ss, p_rs, o_ss, o_rs, met,
 ):
     dp = lax.axis_index("dp")
     z = lax.axis_index("tensor")
@@ -97,20 +108,19 @@
         pltpu.make_async_copy(ref, ref, sem).wait()
 
     def g_copy(k):
-        part = pl.ds((k % CH) * 4 * RQ, 4 * RQ)
-        return pltpu.make_async_copy(grads.at[k // CH, :, :, :, part, :], graw.at[k], g_sem.at[k])
+        l = STARTS[k] // UT
+        part = pl.ds(STARTS[k] % UT * UR, SIZES[k] * UR)
+        return pltpu.make_async_copy(
+            grads.at[l, :, :, :, part, :], graw.at[l, :, :, :, part, :], g_sem.at[k]
+        )
 
     for k in range(AHEAD):
         g_copy(k).start()
     barrier = pltpu.get_barrier_semaphore()
 
-    def greet(i, carry):
-        pl.semaphore_signal(barrier, inc=1, device_id=dev(i // 8, (i // 2) % 4, i % 2), device_id_type=MESH)
-        return carry
-
-    lax.fori_loop(1, 32, greet, 0)
-    for dz in range(1, 4):
-        pl.semaphore_signal(barrier, inc=1, device_id=dev(dz=dz), device_id_type=MESH)
+    near = (dev(dc=1), dev(dx=1), dev(dx=3), dev(dy=1), dev(dy=3), dev(dz=1), dev(dz=3))
+    for target in near:
+        pl.semaphore_signal(barrier, inc=1, device_id=target, device_id_type=MESH)
 
     ins = [
         pltpu.make_async_copy(a, b, in_sem.at[i])
@@ -129,12 +139,18 @@
             for copy in ins:
                 copy.start()
 
+    def units(k):
+        return pl.ds(STARTS[k], SIZES[k])
+
     def spread(k, core, write):
+        l = STARTS[k] // UT
+
         def step(i, carry):
             a, b = i // 4, i % 4
-            v = graw[k, a, b, core].astype(F32)
-            for q in range(4):
-                write(q, a if q < 2 else b, b if q < 2 else a, v[q * RQ:(q + 1) * RQ, :])
+            for u in range(STARTS[k], STARTS[k] + SIZES[k]):
+                v = graw[l, a, b, core, pl.ds(u % UT * UR, UR), :].astype(F32)
+                for q in range(4):
+                    write(u, q, a if q < 2 else b, b if q < 2 else a, v[q * RQ:(q + 1) * RQ, :])
             return carry
 
         lax.fori_loop(0, 16, step, 0)
@@ -143,78 +159,82 @@
         g_copy(k).wait()
         load_more(k)
 
-        def write(q, i, j, v):
-            stage[k, q, i, j] = v
+        def write(u, q, i, j, v):
+            stage[u, q, i, j] = v
 
         spread(k, 1 - c, write)
         if k == 0:
-            pl.semaphore_wait(barrier, 34)
-        send(stage.at[k], acc.at[k], s_sem.at[0], d_rs.at[k], dev(dc=1))
+            pl.semaphore_wait(barrier, 7)
+        send(stage.at[units(k)], acc.at[units(k)], s_sem.at[0], d_rs.at[k], dev(dc=1))
 
     first = (x, y)
     second = (y, x)
     ways = ((dev(dx=1), dev(dx=3)), (dev(dy=1), dev(dy=3)))
 
     def stage_1(k):
-        wait_all(acc.at[k], d_rs.at[k])
-
-        def write(q, i, j, v):
-            acc[k, q, i, j] += v
+        wait_all(acc.at[units(k)], d_rs.at[k])
+
+        def write(u, q, i, j, v):
+            acc[u, q, i, j] += v
 
         spread(k, c, write)
+        un = units(k)
         for h in range(2):
             i0, (plus, minus), qa, qb = first[h], ways[h], 2 * h, 2 * h + 1
-            send(acc.at[k, qa, (i0 + 2) % 4], r1a.at[k, qa], s_sem.at[1], r1a_rs.at[k], plus)
-            send(acc.at[k, qb, (i0 + 2) % 4], r1a.at[k, qb], s_sem.at[1], r1a_rs.at[k], minus)
+            send(acc.at[un, qa, (i0 + 2) % 4], r1a.at[un, qa], s_sem.at[1], r1a_rs.at[k], plus)
+            send(acc.at[un, qb, (i0 + 2) % 4], r1a.at[un, qb], s_sem.at[1], r1a_rs.at[k], minus)
         for h in range(2):
             i0, (plus, minus), qa, qb = first[h], ways[h], 2 * h, 2 * h + 1
-            send(acc.at[k, qb, (i0 + 1) % 4], r1b.at[k, qb, 0], s_sem.at[2], r1b_rs.at[k], plus)
-            send(acc.at[k, qa, (i0 + 3) % 4], r1b.at[k, qa, 1], s_sem.at[2], r1b_rs.at[k], minus)
+            send(acc.at[un, qb, (i0 + 1) % 4], r1b.at[un, qb, 0], s_sem.at[2], r1b_rs.at[k], plus)
+            send(acc.at[un, qa, (i0 + 3) % 4], r1b.at[un, qa, 1], s_sem.at[2], r1b_rs.at[k], minus)
 
     def stage_2(k):
-        wait_all(r1a.at[k], r1a_rs.at[k])
+        un = units(k)
+        wait_all(r1a.at[un], r1a_rs.at[k])
         for h in range(2):
             i0, (plus, minus), qa, qb = first[h], ways[h], 2 * h, 2 * h + 1
-            acc[k, qa, (i0 + 1) % 4] += r1a[k, qa]
-            send(acc.at[k, qa, (i0 + 1) % 4], r1b.at[k, qa, 0], s_sem.at[2], r1b_rs.at[k], plus)
-            acc[k, qb, (i0 + 3) % 4] += r1a[k, qb]
-            send(acc.at[k, qb, (i0 + 3) % 4], r1b.at[k, qb, 1], s_sem.at[2], r1b_rs.at[k], minus)
+            acc[un, qa, (i0 + 1) % 4] += r1a[un, qa]
+            send(acc.at[un, qa, (i0 + 1) % 4], r1b.at[un, qa, 0], s_sem.at[2], r1b_rs.at[k], plus)
+            acc[un, qb, (i0 + 3) % 4] += r1a[un, qb]
+            send(acc.at[un, qb, (i0 + 3) % 4], r1b.at[un, qb, 1], s_sem.at[2], r1b_rs.at[k], minus)
 
     def stage_3(k):
-        wait_all(r1b.at[k], r1b_rs.at[k])
+        un = units(k)
+        wait_all(r1b.at[un], r1b_rs.at[k])
         for h in range(2):
             i0, j0, (plus, minus), qa, qb = first[h], second[h], ways[1 - h], 2 * h, 2 * h + 1
             for q in (qa, qb):
-                acc[k, q, i0] += r1b[k, q, 0] + r1b[k, q, 1]
-            send(acc.at[k, qa, i0, (j0 + 2) % 4], r2a.at[k, qa], s_sem.at[3], r2a_rs.at[k], plus)
-            send(acc.at[k, qb, i0, (j0 + 2) % 4], r2a.at[k, qb], s_sem.at[3], r2a_rs.at[k], minus)
-            send(acc.at[k, qb, i0, (j0 + 1) % 4], r2b.at[k, qb, 0], s_sem.at[4], r2b_rs.at[k], plus)
-            send(acc.at[k, qa, i0, (j0 + 3) % 4], r2b.at[k, qa, 1], s_sem.at[4], r2b_rs.at[k], minus)
+                acc[un, q, i0] += r1b[un, q, 0] + r1b[un, q, 1]
+            send(acc.at[un, qa, i0, (j0 + 2) % 4], r2a.at[un, qa], s_sem.at[3], r2a_rs.at[k], plus)
+            send(acc.at[un, qb, i0, (j0 + 2) % 4], r2a.at[un, qb], s_sem.at[3], r2a_rs.at[k], minus)
+            send(acc.at[un, qb, i0, (j0 + 1) % 4], r2b.at[un, qb, 0], s_sem.at[4], r2b_rs.at[k], plus)
+            send(acc.at[un, qa, i0, (j0 + 3) % 4], r2b.at[un, qa, 1], s_sem.at[4], r2b_rs.at[k], minus)
 
     def stage_4(k):
-        wait_all(r2a.at[k], r2a_rs.at[k])
+        un = units(k)
+        wait_all(r2a.at[un], r2a_rs.at[k])
         for h in range(2):
             i0, j0, (plus, minus), qa, qb = first[h], second[h], ways[1 - h], 2 * h, 2 * h + 1
-            acc[k, qa, i0, (j0 + 1) % 4] += r2a[k, qa]
-            send(acc.at[k, qa, i0, (j0 + 1) % 4], r2b.at[k, qa, 0], s_sem.at[4], r2b_rs.at[k], plus)
-            acc[k, qb, i0, (j0 + 3) % 4] += r2a[k, qb]
-            send(acc.at[k, qb, i0, (j0 + 3) % 4], r2b.at[k, qb, 1], s_sem.at[4], r2b_rs.at[k], minus)
+            acc[un, qa, i0, (j0 + 1) % 4] += r2a[un, qa]
+            send(acc.at[un, qa, i0, (j0 + 1) % 4], r2b.at[un, qa, 0], s_sem.at[4], r2b_rs.at[k], plus)
+            acc[un, qb, i0, (j0 + 3) % 4] += r2a[un, qb]
+            send(acc.at[un, qb, i0, (j0 + 3) % 4], r2b.at[un, qb, 1], s_sem.at[4], r2b_rs.at[k], minus)
 
     def stage_5(k):
-        l = k // CH
-        wait_all(r2b.at[k], r2b_rs.at[k])
-        for q in range(4):
-            h = q // 2
-            span = pl.ds((k % CH) * 4 * RQ + q * RQ, RQ)
-            g = acc[k, q, first[h], second[h]] + r2b[k, q, 0] + r2b[k, q, 1]
-            gsum[l, span, :] = g
-            sq = g * g
-            rowrep[l, span, :] = jnp.broadcast_to(jnp.sum(sq, 1, keepdims=True), (RQ, 128))
-            colacc[l] += jnp.sum(sq.reshape(RQ // 8, 8, CB), 0)
-            for n in range(3):
-                m = DECAYS[n] * v_moms[n, l, span, :] + (np.float32(1) - DECAYS[n]) * g
-                n_moms[n, l, span, :] = m
-                macc[l, n] += jnp.sum((m * m).reshape(RQ // 8, 8, CB), 0)
+        l = STARTS[k] // UT
+        wait_all(r2b.at[units(k)], r2b_rs.at[k])
+        for u in range(STARTS[k], STARTS[k] + SIZES[k]):
+            for q in range(4):
+                span = pl.ds(u % UT * UR + q * RQ, RQ)
+                g = acc[u, q, first[q // 2], second[q // 2]] + r2b[u, q, 0] + r2b[u, q, 1]
+                gsum[l, span, :] = g
+                sq = g * g
+                rowrep[l, span, :] = jnp.broadcast_to(jnp.sum(sq, 1, keepdims=True), (RQ, 128))
+                colacc[l] += sq
+                for n in range(3):
+                    m = DECAYS[n] * v_moms[n, l, span, :] + (np.float32(1) - DECAYS[n]) * g
+                    n_moms[n, l, span, :] = m
+                    macc[l, n] += m * m
 
     lane = lax.broadcasted_iota(jnp.int32, (1, 128), 1)
 
@@ -273,35 +293,48 @@
     def pick(row, j):
         return jnp.sum(jnp.where(lane == j, row, 0.0), 1, keepdims=True)
 
-    def z_send(l):
+    def exchange(l):
+        sums = [colacc[l], macc[l, 0], macc[l, 1], macc[l, 2], pacc[l]]
+        pa[l, :, 0:128] = put([total(v) for v in sums] + [jnp.sum(v_row[l:l + 1, :], 1, keepdims=True)])
+        pa[l, :, 128:384] = jnp.sum(colacc[l], 0, keepdims=True)
+        send(pa.at[l], cr.at[l], c_ss.at[l], c_rs.at[l], dev(dc=1))
         for i in range(2):
-            zs[l, :, i * 128:(i + 1) * 128] = rows_to_lane(rowrep[l, i * 128:(i + 1) * 128, :])
-        zs[l, :, 256:384] = put([total(colacc[l]), total(macc[l, 0]), total(macc[l, 1]), total(macc[l, 2]), total(pacc[l])])
+            zb[l, :, (i + 1) * 128:(i + 2) * 128] = rows_to_lane(rowrep[l, i * 128:(i + 1) * 128, :])
+
+    def announce(l):
+        wait_all(cr.at[l], c_rs.at[l])
+        pb[l] = pa[l] + cr[l]
+        zb[l, :, 0:128] = pb[l, :, 0:128]
+
+        def other(i, carry):
+            j = i % 15 + 1
+            target = dev(j // 4, j % 4, 0, 1 + (1 + i // 15) % 3)
+            send(pb.at[l, :, pl.ds(0, 128)], sr.at[l, i], o_ss.at[l], o_rs.at[l], target)
+            return carry
+
+        def plane(j, carry):
+            send(pb.at[l], pr.at[l, j - 1], p_ss.at[l], p_rs.at[l], dev(j // 4, j % 4))
+            return carry
+
+        lax.fori_loop(0, 15, other, 0)
+        lax.fori_loop(1, 16, plane, 0)
+        lax.fori_loop(15, 45, other, 0)
         for dz in range(1, 4):
-            send(zs.at[l], zr.at[l, dz - 1], z_ss.at[l], z_rs.at[l], dev(dz=dz))
-
-    def p_send(l):
+            send(zb.at[l], zr.at[l, dz - 1], z_ss.at[l], z_rs.at[l], dev(dz=dz))
+
+    def control(l):
         wait_all(zr.at[l], z_rs.at[l])
-        got = zs[l] + zr[l, 0] + zr[l, 1] + zr[l, 2]
-        new = 0.9 * v_row[l:l + 1, :] + 0.1 * got[:, 0:256] / KV
+        got = zb[l] + zr[l, 0] + zr[l, 1] + zr[l, 2]
+        new = 0.9 * v_row[l:l + 1, :] + 0.1 * got[:, 128:384] / KV
         n_rows[l:l + 1, :] = new
-        ps[l, :, 0:256] = jnp.sum(colacc[l], 0, keepdims=True)
-        ps[l, :, 256:384] = got[:, 256:384] + jnp.where(lane == 5, jnp.sum(new, 1, keepdims=True), 0.0)
-
-        def out(i, carry):
-            send(ps.at[l], pr.at[l, i - 1], p_ss.at[l], p_rs.at[l], dev(i // 8, (i // 2) % 4, i % 2))
-            return carry
-
-        lax.fori_loop(1, 32, out, 0)
         for i in range(2):
             rowrep[l, i * 128:(i + 1) * 128, :] = lane_to_rows(new[:, i * 128:(i + 1) * 128])
-
-    def control(l):
         wait_all(pr.at[l], p_rs.at[l])
-        got = ps[l] + jnp.sum(pr[l], 0)
-        new = 0.9 * v_col[l:l + 1, :] + 0.1 * got[:, 0:256] / D
+        near = jnp.sum(pr[l], 0)
+        new = 0.9 * v_col[l:l + 1, :] + 0.1 * (pb[l, :, 128:384] + near[:, 128:384]) / D
         n_cols[l:l + 1, :] = new
-        sums = got[:, 256:384]
+        wait_all(sr.at[l], o_rs.at[l])
+        sums = got[:, 0:128] + near[:, 0:128] + jnp.sum(sr[l], 0)
         means = sums / (D * KV)
         stats = jnp.log(means + 1e-06)
         gates = pre[l]
@@ -324,7 +357,7 @@
         side = wst[l, :, 128:256].astype(F32)
         side = jnp.where(lane == 16, high, jnp.where(lane == 17, bias - high, side))
         wst[l, :, 128:256] = side.astype(BF16)
-        row_mean = pick(sums, 5) / D
+        row_mean = (0.9 * (pick(sums, 5) / 4) + 0.1 * pick(sums, 0) / KV) / D
         colrow[l] = new / row_mean
         norms[l, 0:1, :] = jnp.broadcast_to(lax.rsqrt(pick(means, 4) + 1e-06), (1, 128))
         norms[l, 1:2, :] = jnp.broadcast_to(lax.rsqrt(pick(means, 0) + 1e-06), (1, 128))
@@ -335,33 +368,31 @@
             norms.at[0], wst.at[0], w2rep, mod.at[0], n_params,
         )
 
-    stage_d(0)
-    stage_d(1)
-    for t in range(NC + 4):
-        if t < NC:
-            stage_1(t)
-        if t + 2 < NC:
-            stage_d(t + 2)
-        if 0 <= t - 1 < NC:
-            stage_2(t - 1)
-        if t == 1:
+    def meet(n):
+        for target in (dev(dz=1), dev(dz=3)):
+            pl.semaphore_signal(met.at[n], inc=1, device_id=target, device_id_type=MESH)
+
+    steps = (stage_d, stage_1, stage_2, stage_3, stage_4, stage_5)
+    for step, k in ORDER:
+        if step == "p":
             prepare()
-        if 0 <= t - 2 < NC:
-            stage_3(t - 2)
-        if 0 <= t - 3 < NC:
-            stage_4(t - 3)
-        if 0 <= t - 4 < NC:
-            stage_5(t - 4)
-        if t == CH + 3:
-            z_send(0)
-        if t == CH + 4:
-            p_send(0)
-        if t == CH + 5:
+        elif step == "x":
+            exchange(0)
+        elif step == "a":
+            pl.semaphore_wait(met.at[1], 2)
+            announce(0)
+        elif step == "c":
             control(0)
-    z_send(1)
-    network_0(0, 2)
-    p_send(1)
-    network_0(2, 4)
+        else:
+            steps[step](k)
+        if step == 5 and k == 0:
+            meet(0)
+        if step == 5 and k == 1:
+            pl.semaphore_wait(met.at[0], 2)
+            meet(1)
+    exchange(1)
+    announce(1)
+    network_0(0, 4)
     control(1)
     wait_all(acc, s_sem.at[0])
     wait_all(r1a, s_sem.at[1])
@@ -369,8 +400,10 @@
     wait_all(r2a, s_sem.at[3])
     wait_all(r2b, s_sem.at[4])
     for l in range(L):
+        wait_all(cr.at[l], c_ss.at[l])
         wait_all(zr.at[l], z_ss.at[l])
         wait_all(pr.at[l], p_ss.at[l])
+        wait_all(sr.at[l], o_ss.at[l])
 
 
 def finish(
@@ -430,13 +463,13 @@
         in_specs=[hbm] * 14,
         out_specs=(held,) * len(between),
         scratch_shapes=[
-            vmem((NC, 4, 4, 2, 4 * RQ, CB), BF16),
-            vmem((NC, 4, 4, 4) + quarter, F32),
-            vmem((NC, 4, 4, 4) + quarter, F32),
-            vmem((NC, 4, 4) + quarter, F32),
-            vmem((NC, 4, 2, 4) + quarter, F32),
-            vmem((NC, 4) + quarter, F32),
-            vmem((NC, 4, 2) + quarter, F32),
+            vmem((L, 4, 4, 2, RB, CB), BF16),
+            vmem((NU, 4, 4, 4) + quarter, F32),
+            vmem((NU, 4, 4, 4) + quarter, F32),
+            vmem((NU, 4, 4) + quarter, F32),
+            vmem((NU, 4, 2, 4) + quarter, F32),
+            vmem((NU, 4) + quarter, F32),
+            vmem((NU, 4, 2) + quarter, F32),
             vmem((3, L, RB, CB), F32),
             vmem((L, RB), F32),
             vmem((L, CB), F32),
@@ -456,22 +489,19 @@
             vmem((L, 1, 4 * H), F32),
             vmem((HID + 2, 128), F32),
             vmem((L, 1, 384), F32),
+            vmem((L, 1, 384), F32),
+            vmem((L, 1, 384), F32),
+            vmem((L, 1, 384), F32),
             vmem((L, 3, 1, 384), F32),
-            vmem((L, 1, 384), F32),
-            vmem((L, 31, 1, 384), F32),
+            vmem((L, 15, 1, 384), F32),
+            vmem((L, 45, 1, 128), F32),
             dma((13,)),
             dma((NC,)),
             dma((5,)),
-            dma((NC,)),
-            dma((NC,)),
-            dma((NC,)),
-            dma((NC,)),
-            dma((NC,)),
-            dma((L,)),
-            dma((L,)),
-            dma((L,)),
-            dma((L,)),
-        ],
+        ]
+        + [dma((NC,))] * 5
+        + [dma((L,))] * 8
+        + [pltpu.SemaphoreType.REGULAR((2,))],
         compiler_params=pltpu.CompilerParams(
             collective_id=0, has_side_effects=True, vmem_limit_bytes=46 * 2**20
         ),

time: 75.9 us -> 68.6 us (0.904)
  Pallas kernels: 75.1 us -> 67.9 us
    pallas_call x1, Pallas kernels: 72.2 us -> 65 us  [body(): pl.pallas_call(kernel, out_shape=between, in_specs=[hbm] * 14, out_specs=...]
where the time goes in v3:
time: 68.6 us; the launch traced here: 68.5 us
  Pallas kernels  67.9 us (99%)
    pallas_call x1, Pallas kernels, body(): pl.pallas_call(kernel, out_shape=between, in_specs=[hbm] * 14, out_specs=...  65 us
    pallas_call x1, Pallas kernels, body(): pl.pallas_call(finish, out_shape=(jax.ShapeDtypeStruct((L, RB, CB), F32),...  2.91 us

profile of v3, /device:TPU:1, one launch (start us, length us, event | category | flops | bytes accessed | tf_op | source)
XLA Modules:
  0.0 68.5 jit_solution(15250762474192471406)
XLA Ops:
  0.6 65.0 %update.1 = (f32[256,256]{1,0:T(8,128)S(1)}, f32[3,2,256,256]{3,2,1,0:T(8,128)S(1)}, f32[2,256,256]{2,1,0:T(8,128)S(1)}, f32[2,256,256]{2,1,0:T(8,128)S(1)}, f32...) custom-call(bf16[2,4,4,2,256,256]{5,4,3,2,1,0:T(8,128)(2,1)} %bitcas, ...), custom_call_target="tpu_custom_call" | custom-call | tf_op jit(solution)/shard_map/update/pallas_call | solution.py:460
  65.6 2.9 %finish.1 = (f32[2,256,256]{2,1,0:T(8,128)}, f32[3,2,256,256]{3,2,1,0:T(8,128)}, f32[2,256]{1,0:T(2,128)}, f32[2,256]{1,0:T(2,128)}, f32[2,512]{1,0:T(2,128)}, /*index=5*/f32[2,512]{1,0:T(2,128)}) custom-call(f32[256,256]{1,0:T(8,128)S(1)} %get-tuple-element.20.params_0, f32[3,2,256,256]{3,2,1,0:T(8,128)S(1)} %get-tuple-element.21.moms, ...), custom_call_target="tpu_custom_call" | custom-call | tf_op jit(solution)/shard_map/finish/pallas_call | solution.py:510

commit v4 on v3

--- a/solution.py
+++ b/solution.py
@@ -21,15 +21,17 @@
 UR = 4 * RQ
 UT = RB // UR
 NU = L * UT
-SIZES = (1, 2, 2, 3, 3, 2, 2, 1)
+SIZES = (1, 2, 2, 3, 3, 3, 2)
 NC = len(SIZES)
 STARTS = tuple(sum(SIZES[:k]) for k in range(NC))
 HALF = STARTS.index(UT)
+DIRECT_1 = NC
+DIRECT_2 = NC - 2
 ORDER = (
-    (0, 0), (0, 1), (0, 2), (1, 0), (1, 1), (1, 2), (2, 0), (0, 3), (2, 1), (0, 4), (1, 3), (3, 1), (2, 2), (0, 5),
-    (2, 3), (0, 6), (1, 4), (0, 7), (3, 0), ("p", 0), (3, 2), (4, 1), (3, 3), (1, 5), (4, 0), (1, 7), (4, 3), (4, 2),
-    (1, 6), (2, 4), (5, 0), (2, 5), (5, 1), (5, 2), (5, 3), ("x", 0), (2, 6), (2, 7), ("a", 0), (3, 4), (3, 5),
-    (3, 6), (3, 7), (4, 4), (4, 5), (4, 6), (4, 7), ("c", 0), (5, 4), (5, 5), (5, 6), (5, 7),
+    (0, 0), (0, 1), (1, 0), (1, 1), (0, 2), (0, 3), (2, 0), (1, 2), (1, 3), (2, 1), (3, 0), (0, 4), (2, 2), ("p", 0),
+    ("p", 1), (0, 5), (2, 3), (1, 4), ("p", 2), (4, 0), (3, 2), (3, 3), (3, 1), (1, 5), ("p", 3), (0, 6), (4, 1),
+    (5, 0), (2, 4), (4, 2), (4, 3), (1, 6), (5, 1), (2, 5), (5, 2), (5, 3), ("x", 0), (2, 6), (3, 4), ("a", 0),
+    (3, 5), (4, 4), (3, 6), ("c", 0), (4, 6), (5, 4), (4, 5), (5, 5), (5, 6),
 )
 MESH = pl.DeviceIdType.MESH
 F32 = jnp.float32
@@ -87,7 +89,7 @@
     n_params, n_moms, v_params, gsum, rowrep, colrow, norms, wst, w2rep, mod, n_rows, n_cols, n_hid, n_cell,
     graw, stage, acc, r1a, r1b, r2a, r2b,
     v_moms, v_row, v_col, v_hid, v_cell, v_iw, v_rw, v_gb, headt, v_hb, v_w1, v_w2,
-    hidrep, colacc, macc, pacc, pre, hbcol, pa, cr, pb, zb, zr, pr, sr,
+    hidrep, recsum, colacc, macc, pacc, pre, hbcol, pa, cr, pb, zb, zr, pr, sr,
     in_sem, g_sem, s_sem, d_rs, r1a_rs, r1b_rs, r2a_rs, r2b_rs, c_ss, c_rs, z_ss, z_rs, p_ss, p_rs, o_ss, o_rs, met,
 ):
     dp = lax.axis_index("dp")
@@ -170,6 +172,7 @@
     first = (x, y)
     second = (y, x)
     ways = ((dev(dx=1), dev(dx=3)), (dev(dy=1), dev(dy=3)))
+    across = (dev(dx=2), dev(dy=2))
 
     def stage_1(k):
         wait_all(acc.at[units(k)], d_rs.at[k])
@@ -179,6 +182,13 @@
 
         spread(k, c, write)
         un = units(k)
+        if k >= DIRECT_1:
+            for h in range(2):
+                i0, (plus, minus), both = first[h], ways[h], pl.ds(2 * h, 2)
+                send(acc.at[un, both, (i0 + 2) % 4], r1a.at[un, both], s_sem.at[1], r1a_rs.at[k], across[h])
+                send(acc.at[un, both, (i0 + 1) % 4], r1b.at[un, both, 0], s_sem.at[2], r1b_rs.at[k], plus)
+                send(acc.at[un, both, (i0 + 3) % 4], r1b.at[un, both, 1], s_sem.at[2], r1b_rs.at[k], minus)
+            return
         for h in range(2):
             i0, (plus, minus), qa, qb = first[h], ways[h], 2 * h, 2 * h + 1
             send(acc.at[un, qa, (i0 + 2) % 4], r1a.at[un, qa], s_sem.at[1], r1a_rs.at[k], plus)
@@ -189,6 +199,8 @@
             send(acc.at[un, qa, (i0 + 3) % 4], r1b.at[un, qa, 1], s_sem.at[2], r1b_rs.at[k], minus)
 
     def stage_2(k):
+        if k >= DIRECT_1:
+            return
         un = units(k)
         wait_all(r1a.at[un], r1a_rs.at[k])
         for h in range(2):
@@ -201,16 +213,29 @@
     def stage_3(k):
         un = units(k)
         wait_all(r1b.at[un], r1b_rs.at[k])
+        if k >= DIRECT_1:
+            wait_all(r1a.at[un], r1a_rs.at[k])
         for h in range(2):
             i0, j0, (plus, minus), qa, qb = first[h], second[h], ways[1 - h], 2 * h, 2 * h + 1
             for q in (qa, qb):
-                acc[un, q, i0] += r1b[un, q, 0] + r1b[un, q, 1]
+                got = r1b[un, q, 0] + r1b[un, q, 1]
+                if k >= DIRECT_1:
+                    got = got + r1a[un, q]
+                acc[un, q, i0] += got
+            if k >= DIRECT_2:
+                both = pl.ds(2 * h, 2)
+                send(acc.at[un, both, i0, (j0 + 2) % 4], r2a.at[un, both], s_sem.at[3], r2a_rs.at[k], across[1 - h])
+                send(acc.at[un, both, i0, (j0 + 1) % 4], r2b.at[un, both, 0], s_sem.at[4], r2b_rs.at[k], plus)
+                send(acc.at[un, both, i0, (j0 + 3) % 4], r2b.at[un, both, 1], s_sem.at[4], r2b_rs.at[k], minus)
+                continue
             send(acc.at[un, qa, i0, (j0 + 2) % 4], r2a.at[un, qa], s_sem.at[3], r2a_rs.at[k], plus)
             send(acc.at[un, qb, i0, (j0 + 2) % 4], r2a.at[un, qb], s_sem.at[3], r2a_rs.at[k], minus)
             send(acc.at[un, qb, i0, (j0 + 1) % 4], r2b.at[un, qb, 0], s_sem.at[4], r2b_rs.at[k], plus)
             send(acc.at[un, qa, i0, (j0 + 3) % 4], r2b.at[un, qa, 1], s_sem.at[4], r2b_rs.at[k], minus)
 
     def stage_4(k):
+        if k >= DIRECT_2:
+            return
         un = units(k)
         wait_all(r2a.at[un], r2a_rs.at[k])
         for h in range(2):
@@ -223,10 +248,14 @@
     def stage_5(k):
         l = STARTS[k] // UT
         wait_all(r2b.at[units(k)], r2b_rs.at[k])
+        if k >= DIRECT_2:
+            wait_all(r2a.at[units(k)], r2a_rs.at[k])
         for u in range(STARTS[k], STARTS[k] + SIZES[k]):
             for q in range(4):
                 span = pl.ds(u % UT * UR + q * RQ, RQ)
                 g = acc[u, q, first[q // 2], second[q // 2]] + r2b[u, q, 0] + r2b[u, q, 1]
+                if k >= DIRECT_2:
+                    g = g + r2a[u, q]
                 gsum[l, span, :] = g
                 sq = g * g
                 rowrep[l, span, :] = jnp.broadcast_to(jnp.sum(sq, 1, keepdims=True), (RQ, 128))
@@ -238,7 +267,7 @@
 
     lane = lax.broadcasted_iota(jnp.int32, (1, 128), 1)
 
-    def prepare():
+    def prepare_0():
         for copy in ins:
             copy.wait()
         colacc[...] = jnp.zeros_like(colacc)
@@ -249,18 +278,30 @@
                 return s + v * v
 
             pacc[l] = lax.fori_loop(0, RB // 8, square, jnp.zeros((8, CB), F32))
+        recsum[...] = jnp.zeros_like(recsum)
         reps = [jnp.concatenate([lane_to_rows(v_hid[l:l + 1, i * 128:(i + 1) * 128]) for i in range(4)], 0) for l in range(L)]
         for l in range(L):
             hidrep[l] = reps[l]
 
+    def recurrent(begin, end):
         def recur(i, sums):
             at = pl.ds(pl.multiple_of(i * 8, 8), 8)
             w = v_rw[at, :]
             return tuple(sums[l] + w * jnp.tile(hidrep[l, at, :], (1, 16)) for l in range(L))
 
-        sums = lax.fori_loop(0, H // 8, recur, tuple(jnp.zeros((8, 4 * H), F32) for _ in range(L)))
+        sums = lax.fori_loop(begin, end, recur, tuple(recsum[l] for l in range(L)))
         for l in range(L):
-            pre[l] = jnp.sum(sums[l], 0, keepdims=True) + v_gb[...]
+            recsum[l] = sums[l]
+
+    def prepare_1():
+        recurrent(0, H // 16)
+
+    def prepare_2():
+        recurrent(H // 16, H // 8)
+        for l in range(L):
+            pre[l] = jnp.sum(recsum[l], 0, keepdims=True) + v_gb[...]
+
+    def prepare_3():
         hbcol[...] = lane_to_rows(jnp.concatenate([v_hb[...], jnp.zeros((1, 126 - HID), F32)], 1))[0:HID + 2, :]
         w1t = jnp.concatenate([v_w1[...], jnp.zeros((128 - NF, HID), F32)], 0)
         w1t = jnp.transpose(jnp.concatenate([w1t, jnp.zeros((128, 128 - HID), F32)], 1))[0:HID, :]
@@ -375,7 +416,7 @@
     steps = (stage_d, stage_1, stage_2, stage_3, stage_4, stage_5)
     for step, k in ORDER:
         if step == "p":
-            prepare()
+            (prepare_0, prepare_1, prepare_2, prepare_3)[k]()
         elif step == "x":
             exchange(0)
         elif step == "a":
@@ -393,12 +434,12 @@
     exchange(1)
     announce(1)
     network_0(0, 4)
-    control(1)
     wait_all(acc, s_sem.at[0])
     wait_all(r1a, s_sem.at[1])
     wait_all(r1b, s_sem.at[2])
     wait_all(r2a, s_sem.at[3])
     wait_all(r2b, s_sem.at[4])
+    control(1)
     for l in range(L):
         wait_all(cr.at[l], c_ss.at[l])
         wait_all(zr.at[l], z_ss.at[l])
@@ -483,6 +524,7 @@
             vmem((NF, HID), F32),
             vmem((2, HID), F32),
             vmem((L, H, 128), F32),
+            vmem((L, 8, 4 * H), F32),
             vmem((L, 8, CB), F32),
             vmem((L, 3, 8, CB), F32),
             vmem((L, 8, CB), F32),

time: 68.6 us -> 67.9 us (0.990)
  Pallas kernels: 67.9 us -> 67.1 us
    pallas_call x1, Pallas kernels: 65 us -> 64.2 us  [body(): pl.pallas_call(kernel, out_shape=between, in_specs=[hbm] * 14, out_specs=...]
where the time goes in v4:
time: 67.9 us; the launch traced here: 67.8 us
  Pallas kernels  67.1 us (99%)
    pallas_call x1, Pallas kernels, body(): pl.pallas_call(kernel, out_shape=between, in_specs=[hbm] * 14, out_specs=...  64.2 us
    pallas_call x1, Pallas kernels, body(): pl.pallas_call(finish, out_shape=(jax.ShapeDtypeStruct((L, RB, CB), F32),...  2.92 us

profile of v4, /device:TPU:1, one launch (start us, length us, event | category | flops | bytes accessed | tf_op | source)
XLA Modules:
  0.0 67.8 jit_solution(8968003713140822962)
XLA Ops:
  0.6 64.2 %update.1 = (f32[256,256]{1,0:T(8,128)S(1)}, f32[3,2,256,256]{3,2,1,0:T(8,128)S(1)}, f32[2,256,256]{2,1,0:T(8,128)S(1)}, f32[2,256,256]{2,1,0:T(8,128)S(1)}, f32...) custom-call(bf16[2,4,4,2,256,256]{5,4,3,2,1,0:T(8,128)(2,1)} %bitcas, ...), custom_call_target="tpu_custom_call" | custom-call | tf_op jit(solution)/shard_map/update/pallas_call | solution.py:501
  64.9 2.9 %finish.1 = (f32[2,256,256]{2,1,0:T(8,128)}, f32[3,2,256,256]{3,2,1,0:T(8,128)}, f32[2,256]{1,0:T(2,128)}, f32[2,256]{1,0:T(2,128)}, f32[2,512]{1,0:T(2,128)}, /*index=5*/f32[2,512]{1,0:T(2,128)}) custom-call(f32[256,256]{1,0:T(8,128)S(1)} %get-tuple-element.20.params_0, f32[3,2,256,256]{3,2,1,0:T(8,128)S(1)} %get-tuple-element.21.moms, ...), custom_call_target="tpu_custom_call" | custom-call | tf_op jit(solution)/shard_map/finish/pallas_call | solution.py:552

commit v5 on v4

--- a/solution.py
+++ b/solution.py
@@ -98,8 +98,13 @@
     y = (dp // 2) % 4
     c = dp % 2
 
+    at_x = [(x + d) % 4 * 8 for d in range(4)]
+    at_y = [(y + d) % 4 * 2 for d in range(4)]
+    at_c = [c, 1 - c]
+    at_z = [(z + d) % 4 for d in range(4)]
+
     def dev(dx=0, dy=0, dc=0, dz=0):
-        return (((x + dx) % 4) * 8 + ((y + dy) % 4) * 2 + (c + dc) % 2, (z + dz) % 4)
+        return (at_x[dx] + at_y[dy] + at_c[dc], at_z[dz])
 
     def send(src, dst, ss, rs, target):
         pltpu.make_async_remote_copy(
@@ -347,19 +352,17 @@
         pb[l] = pa[l] + cr[l]
         zb[l, :, 0:128] = pb[l, :, 0:128]
 
-        def other(i, carry):
-            j = i % 15 + 1
-            target = dev(j // 4, j % 4, 0, 1 + (1 + i // 15) % 3)
-            send(pb.at[l, :, pl.ds(0, 128)], sr.at[l, i], o_ss.at[l], o_rs.at[l], target)
-            return carry
-
-        def plane(j, carry):
+        def others(n, dz):
+            for j in range(1, 16):
+                send(
+                    pb.at[l, :, pl.ds(0, 128)], sr.at[l, 15 * n + j - 1], o_ss.at[l], o_rs.at[l], dev(j // 4, j % 4, 0, dz)
+                )
+
+        others(0, 2)
+        for j in range(1, 16):
             send(pb.at[l], pr.at[l, j - 1], p_ss.at[l], p_rs.at[l], dev(j // 4, j % 4))
-            return carry
-
-        lax.fori_loop(0, 15, other, 0)
-        lax.fori_loop(1, 16, plane, 0)
-        lax.fori_loop(15, 45, other, 0)
+        others(1, 3)
+        others(2, 1)
         for dz in range(1, 4):
             send(zb.at[l], zr.at[l, dz - 1], z_ss.at[l], z_rs.at[l], dev(dz=dz))
 

time: 67.9 us -> 67 us (0.987)
  Pallas kernels: 67.1 us -> 66.2 us
    pallas_call x1, Pallas kernels: 64.2 us -> 63.3 us  [body(): pl.pallas_call(kernel, out_shape=between, in_specs=[hbm] * 14, out_specs=...]
where the time goes in v5:
time: 67 us; the launch traced here: 66.9 us
  Pallas kernels  66.2 us (99%)
    pallas_call x1, Pallas kernels, body(): pl.pallas_call(kernel, out_shape=between, in_specs=[hbm] * 14, out_specs=...  63.3 us
    pallas_call x1, Pallas kernels, body(): pl.pallas_call(finish, out_shape=(jax.ShapeDtypeStruct((L, RB, CB), F32),...  2.91 us

profile of v5, /device:TPU:1, one launch (start us, length us, event | category | flops | bytes accessed | tf_op | source)
XLA Modules:
  0.0 66.9 jit_solution(2554815309422084816)
XLA Ops:
  0.6 63.3 %update.1 = (f32[256,256]{1,0:T(8,128)S(1)}, f32[3,2,256,256]{3,2,1,0:T(8,128)S(1)}, f32[2,256,256]{2,1,0:T(8,128)S(1)}, f32[2,256,256]{2,1,0:T(8,128)S(1)}, f32...) custom-call(bf16[2,4,4,2,256,256]{5,4,3,2,1,0:T(8,128)(2,1)} %bitcas, ...), custom_call_target="tpu_custom_call" | custom-call | tf_op jit(solution)/shard_map/update/pallas_call | solution.py:504
  64.0 2.9 %finish.1 = (f32[2,256,256]{2,1,0:T(8,128)}, f32[3,2,256,256]{3,2,1,0:T(8,128)}, f32[2,256]{1,0:T(2,128)}, f32[2,256]{1,0:T(2,128)}, f32[2,512]{1,0:T(2,128)}, /*index=5*/f32[2,512]{1,0:T(2,128)}) custom-call(f32[256,256]{1,0:T(8,128)S(1)} %get-tuple-element.20.params_0, f32[3,2,256,256]{3,2,1,0:T(8,128)S(1)} %get-tuple-element.21.moms, ...), custom_call_target="tpu_custom_call" | custom-call | tf_op jit(solution)/shard_map/finish/pallas_call | solution.py:555

commit v6 on v5

--- a/solution.py
+++ b/solution.py
@@ -89,7 +89,7 @@
     n_params, n_moms, v_params, gsum, rowrep, colrow, norms, wst, w2rep, mod, n_rows, n_cols, n_hid, n_cell,
     graw, stage, acc, r1a, r1b, r2a, r2b,
     v_moms, v_row, v_col, v_hid, v_cell, v_iw, v_rw, v_gb, headt, v_hb, v_w1, v_w2,
-    hidrep, recsum, colacc, macc, pacc, pre, hbcol, pa, cr, pb, zb, zr, pr, sr,
+    hidrep, recsum, colacc, macc, early, pre, hbcol, pa, cr, pb, zb, zr, pr, sr,
     in_sem, g_sem, s_sem, d_rs, r1a_rs, r1b_rs, r2a_rs, r2b_rs, c_ss, c_rs, z_ss, z_rs, p_ss, p_rs, o_ss, o_rs, met,
 ):
     dp = lax.axis_index("dp")
@@ -282,7 +282,9 @@
                 v = v_params[l, pl.ds(pl.multiple_of(i * 8, 8), 8), :]
                 return s + v * v
 
-            pacc[l] = lax.fori_loop(0, RB // 8, square, jnp.zeros((8, CB), F32))
+            squares = lax.fori_loop(0, RB // 8, square, jnp.zeros((8, CB), F32))
+            zero = jnp.zeros((1, 1), F32)
+            early[l] = put([zero] * 4 + [total(squares), jnp.sum(v_row[l:l + 1, :], 1, keepdims=True)])
         recsum[...] = jnp.zeros_like(recsum)
         reps = [jnp.concatenate([lane_to_rows(v_hid[l:l + 1, i * 128:(i + 1) * 128]) for i in range(4)], 0) for l in range(L)]
         for l in range(L):
@@ -340,8 +342,8 @@
         return jnp.sum(jnp.where(lane == j, row, 0.0), 1, keepdims=True)
 
     def exchange(l):
-        sums = [colacc[l], macc[l, 0], macc[l, 1], macc[l, 2], pacc[l]]
-        pa[l, :, 0:128] = put([total(v) for v in sums] + [jnp.sum(v_row[l:l + 1, :], 1, keepdims=True)])
+        sums = [colacc[l], macc[l, 0], macc[l, 1], macc[l, 2]]
+        pa[l, :, 0:128] = early[l] + put([total(v) for v in sums])
         pa[l, :, 128:384] = jnp.sum(colacc[l], 0, keepdims=True)
         send(pa.at[l], cr.at[l], c_ss.at[l], c_rs.at[l], dev(dc=1))
         for i in range(2):
@@ -530,7 +532,7 @@
             vmem((L, 8, 4 * H), F32),
             vmem((L, 8, CB), F32),
             vmem((L, 3, 8, CB), F32),
-            vmem((L, 8, CB), F32),
+            vmem((L, 1, 128), F32),
             vmem((L, 1, 4 * H), F32),
             vmem((HID + 2, 128), F32),
             vmem((L, 1, 384), F32),

time: 67 us -> 67 us (level)
  no operation moved by 1% of the time
where the time goes in v6:
time: 67 us; the launch traced here: 66.9 us
  Pallas kernels  66.2 us (99%)
    pallas_call x1, Pallas kernels, body(): pl.pallas_call(kernel, out_shape=between, in_specs=[hbm] * 14, out_specs=...  63.3 us
    pallas_call x1, Pallas kernels, body(): pl.pallas_call(finish, out_shape=(jax.ShapeDtypeStruct((L, RB, CB), F32),...  2.92 us

profile of v6, /device:TPU:1, one launch (start us, length us, event | category | flops | bytes accessed | tf_op | source)
XLA Modules:
  0.0 66.9 jit_solution(16617129947423871675)
XLA Ops:
  0.6 63.3 %update.1 = (f32[256,256]{1,0:T(8,128)S(1)}, f32[3,2,256,256]{3,2,1,0:T(8,128)S(1)}, f32[2,256,256]{2,1,0:T(8,128)S(1)}, f32[2,256,256]{2,1,0:T(8,128)S(1)}, f32...) custom-call(bf16[2,4,4,2,256,256]{5,4,3,2,1,0:T(8,128)(2,1)} %bitcas, ...), custom_call_target="tpu_custom_call" | custom-call | tf_op jit(solution)/shard_map/update/pallas_call | solution.py:506
  64.0 2.9 %finish.1 = (f32[2,256,256]{2,1,0:T(8,128)}, f32[3,2,256,256]{3,2,1,0:T(8,128)}, f32[2,256]{1,0:T(2,128)}, f32[2,256]{1,0:T(2,128)}, f32[2,512]{1,0:T(2,128)}, /*index=5*/f32[2,512]{1,0:T(2,128)}) custom-call(f32[256,256]{1,0:T(8,128)S(1)} %get-tuple-element.20.params_0, f32[3,2,256,256]{3,2,1,0:T(8,128)S(1)} %get-tuple-element.21.moms, ...), custom_call_target="tpu_custom_call" | custom-call | tf_op jit(solution)/shard_map/finish/pallas_call | solution.py:557
